TPU v7x, 256 devices: a whole 4x4x8 slice. The times are simulated.
256 devices in a mesh: loop: 64 (over y, x_hi, z), layer: 4 (over x_lo, core).
Axes of the slice: x: 4 (x_hi: 2, x_lo: 2; x = x_hi * 2 + x_lo), y: 4, z: 8, core: 2. Of those that a mesh axis runs over, the one named last changes fastest.
Arguments:
- queries: bfloat16 [8192, 768], P('loop'), may hold values from -8 to 8, as said below
- candidates: bfloat16 [32768, 768], P(('loop', 'layer')), may hold values from -8 to 8, as said below
- cand_ids: int32 [32768], P(('loop', 'layer')), may hold values from 0 to 32767, each once
Outputs:
- near_dist: float32 [8192, 32], P(('loop', 'layer'))
- near_ids: int32 [8192, 32], P(('loop', 'layer'))
Inputs may be any that keep to these rules, and one draw needn't show every extreme that they name: `queries`: every entry is a whole number. `candidates`: every entry is a whole number.
All inputs are finite; a program needn't handle non-finite values.
Results may differ from a plain program's by a relative error of at most 0.0003.
Values may be sent and summed in bfloat16 or wider, within the bound.
A program may use at most 64 MiB of HBM per device.

v0:
```python
import jax
import jax.numpy as jnp
from jax import lax
from jax.sharding import PartitionSpec as P

D = 768
K = 32
STEPS = 4


def from_behind(value, axis, steps):
    count = lax.axis_size(axis)
    pairs = [(source, (source + steps) % count) for source in range(count)]
    return lax.ppermute(value, axis, pairs)


def combined_all(value, axis, join):
    pieces = jax.tree.map(lambda part: lax.all_gather(part, axis), value)
    head = jax.tree.map(lambda part: part[0], pieces)
    tail = jax.tree.map(lambda part: part[1:], pieces)
    so_far, _ = lax.scan(lambda so_far, share: (join(so_far, share), None), head, tail)
    return so_far


def select(dist, ids, count):
    ordered = lax.sort((dist, ids), dimension=1, num_keys=2)
    return (ordered[0][:, :count], ordered[1][:, :count])


def order_list(dist, ids):
    return lax.sort((dist, ids), dimension=1, num_keys=2)


def row_norms(block):
    return jnp.sum(jnp.square(block.astype(jnp.float32)), 1)


def block_list(block, query_norm, chosen, chosen_ids):
    cand_norm = row_norms(chosen)
    inner = jnp.einsum("qd,cd->qc", block, chosen, preferred_element_type=jnp.float32)
    dist = query_norm[:, None] + cand_norm[None, :] - 2.0 * inner
    every_id = jnp.broadcast_to(chosen_ids[None, :], dist.shape)
    return select(dist, every_id, K)


def join(first, second):
    dist = jnp.concatenate([first[0], second[0]], 1)
    ids = jnp.concatenate([first[1], second[1]], 1)
    return select(dist, ids, K)


def shards(queries, candidates, cand_ids):
    query_norm = row_norms(queries)
    best = block_list(queries, query_norm, candidates, cand_ids)
    moving = (candidates, cand_ids)
    for step in range(STEPS):
        moving = from_behind((moving[0], moving[1]), "loop", 1)
        best = join(best, block_list(queries, query_norm, moving[0], moving[1]))
    rows = queries.shape[0] // lax.axis_size("layer")
    merged = combined_all((best[0], best[1]), "layer", join)
    start = lax.axis_index("layer") * rows
    final_dist = lax.dynamic_slice_in_dim(merged[0], start, rows, 0)
    final_ids = lax.dynamic_slice_in_dim(merged[1], start, rows, 0)
    final_dist, final_ids = order_list(final_dist, final_ids)
    return (final_dist * (0.125 / D), final_ids)


def solution(mesh):
    return jax.shard_map(
        shards,
        mesh=mesh,
        in_specs=(P("loop", None), P(("loop", "layer"), None), P(("loop", "layer"))),
        out_specs=(P(("loop", "layer"), None), P(("loop", "layer"), None)),
        check_vma=False,
    )
```

profile of v0, /device:TPU:1, one launch (start us, length us, event | category | flops | bytes accessed | tf_op | source)
XLA Modules:
  0.0 105.4 jit_solution(6388597055365229722)
XLA Ops:
  0.6 2.5 %collective-permute-start = (bf16[128,768]{1,0:T(8,128)(2,1)}, bf16[128,768]{1,0:T(8,128)(2,1)S(1)}, u32[]{:S(2)}, u32[]{:S(2)}) collective-permute-start(bf16[128,768]{1,0:T(8,128)(2,1)} %param.6), channel_id=1, source_target_pairs={{0,4},{4,8},{8,12},{12,16},{16,20},{20,24},{24,28},{28,32},{32,36}... | collective-permute-start | bytes 589832 | tf_op jit(solution)/shard_map/ppermute | solution.py:14
  3.2 1.6 %collective-permute-start.1 = (s32[128]{0:T(128)}, s32[128]{0:T(128)S(1)}, u32[]{:S(2)}, u32[]{:S(2)}) collective-permute-start(s32[128]{0:T(128)} %param.7), channel_id=1, source_target_pairs={{0,4},{4,8},{8,12},{12,16},{16,20},{20,24},{24,28},{28,32},{32,36}... | collective-permute-start | bytes 1544 | tf_op jit(solution)/shard_map/ppermute | solution.py:14
  4.8 1.2 %multiply_reduce_fusion.4 = (f32[128]{0:T(128)S(1)}, f32[128]{0:T(128)S(1)}) fusion(bf16[128,768]{1,0:T(8,128)(2,1)} %param.6, bf16[128,768]{1,0:T(8,128)(2,1)} %param.5), kind=kLoop, calls=%fused_computation.14 | loop fusion | flops 589568 | bytes 394240 | tf_op jit(solution)/shard_map/reduce_sum | solution.py:35
  6.0 10.9 %collective-permute-done.1 = s32[128]{0:T(128)S(1)} collective-permute-done((s32[128]{0:T(128)}, s32[128]{0:T(128)S(1)}, u32[]{:S(2)}, u32[]{:S(2)}) %collective-permute-start.1) | collective-permute-done | bytes 544 | tf_op jit(solution)/shard_map/ppermute | solution.py:14
  16.9 0.2 fusion
  17.1 0.1 copy.21
  17.2 0.6 copy-done.4
  17.9 0.1 broadcast_in_dim.10.clone
  17.9 2.6 %sort.253 = (f32[128,128]{0,1:T(8,128)S(1)}, s32[128,128]{0,1:T(8,128)S(1)}, s32[128,128]{0,1:T(8,128)}) sort(f32[128,128]{0,1:T(8,128)S(1)} %copy.21, s32[128,128]{0,1:T(8,128)S(1)} %broadcast_in_dim.10.clone, s32[128,128]{0,1:T(8,128)S(1)} %iota.33.clone), dimensions={1}, to_apply=%region_2.0 | sort | flops 229376 | bytes 393216 | tf_op jit(solution)/shard_map/sort | solution.py:26
  20.5 0.1 copy.25
  20.6 0.1 copy.24
  20.7 4.3 %collective-permute-done.3 = s32[128]{0:T(128)S(1)} collective-permute-done((s32[128]{0:T(128)S(1)}, s32[128]{0:T(128)S(1)}, u32[]{:S(2)}, u32[]{:S(2)}) %collective-permute-start.3) | collective-permute-done | bytes 544 | tf_op jit(solution)/shard_map/ppermute | solution.py:14
  25.0 8.1 %collective-permute-done.5 = s32[128]{0:T(128)S(1)} collective-permute-done((s32[128]{0:T(128)S(1)}, s32[128]{0:T(128)S(1)}, u32[]{:S(2)}, u32[]{:S(2)}) %collective-permute-start.5) | collective-permute-done | bytes 544 | tf_op jit(solution)/shard_map/ppermute | solution.py:14
  33.1 0.1 multiply_reduce_fusion.3
  33.2 0.2 add_subtract_fusion.3
  33.5 0.1 copy.27
  33.6 0.1 broadcast_in_dim.11.clone
  33.6 2.6 %sort.254 = (f32[128,128]{0,1:T(8,128)S(1)}, s32[128,128]{0,1:T(8,128)S(1)}, s32[128,128]{0,1:T(8,128)}) sort(f32[128,128]{0,1:T(8,128)S(1)} %copy.27, s32[128,128]{0,1:T(8,128)S(1)} %broadcast_in_dim.11.clone, s32[128,128]{0,1:T(8,128)S(1)} %iota.33.clone), dimensions={1}, to_apply=%region_4.0 | sort | flops 229376 | bytes 393216 | tf_op jit(solution)/shard_map/sort | solution.py:26
  36.2 0.1 copy.31
  36.3 0.3 collective-permute-start.2
  36.6 0.1 pad_add_fusion.1
  36.7 0.1 copy.10
  36.7 0.1 copy.30
  36.8 0.1 pad_maximum_fusion.1
  36.9 0.1 copy.9
  37.0 1.4 %sort.255 = (f32[128,64]{0,1:T(8,128)S(1)}, s32[128,64]{0,1:T(8,128)S(1)}, s32[128,64]{0,1:T(8,128)}) sort(f32[128,64]{0,1:T(8,128)S(1)} %copy.9, s32[128,64]{0,1:T(8,128)S(1)} %copy.10, s32[128,64]{0,1:T(8,128)S(1)} %iota.35), dimensions={1}, to_apply=%region_5.0 | sort | flops 106496 | bytes 196608 | tf_op jit(solution)/shard_map/sort | solution.py:26
  38.4 8.4 %collective-permute-done.2 = bf16[128,768]{1,0:T(8,128)(2,1)S(1)} collective-permute-done((bf16[128,768]{1,0:T(8,128)(2,1)S(1)}, bf16[128,768]{1,0:T(8,128)(2,1)S(1)}, u32[]{:S(2)}, u32[]{:S(2)}) %collective-permute-start.2) | collective-permute-done | bytes 196640 | tf_op jit(solution)/shard_map/ppermute | solution.py:14
  46.8 0.1 multiply_reduce_fusion.2
  46.9 0.2 add_subtract_fusion.2
  47.2 0.1 copy.33
  47.3 0.1 broadcast_in_dim.12.clone
  47.3 2.6 %sort.256 = (f32[128,128]{0,1:T(8,128)S(1)}, s32[128,128]{0,1:T(8,128)S(1)}, s32[128,128]{0,1:T(8,128)}) sort(f32[128,128]{0,1:T(8,128)S(1)} %copy.33, s32[128,128]{0,1:T(8,128)S(1)} %broadcast_in_dim.12.clone, s32[128,128]{0,1:T(8,128)S(1)} %iota.33.clone), dimensions={1}, to_apply=%region_7.0 | sort | flops 229376 | bytes 393216 | tf_op jit(solution)/shard_map/sort | solution.py:26
  50.0 1.4 %sort.257 = (f32[128,64]{0,1:T(8,128)S(1)}, s32[128,64]{0,1:T(8,128)S(1)}, s32[128,64]{0,1:T(8,128)}) sort(f32[128,64]{0,1:T(8,128)S(1)} %pad_maximum_fusion.2, s32[128,64]{0,1:T(8,128)S(1)} %pad_add_fusion.2, s32[128,64]{0,1:T(8,128)S(1)} %iota.37), dimensions={1}, to_apply=%region_8.0 | sort | flops 106496 | bytes 196608 | tf_op jit(solution)/shard_map/sort | solution.py:26
  51.4 8.8 %collective-permute-done.4 = bf16[128,768]{1,0:T(8,128)(2,1)S(1)} collective-permute-done((bf16[128,768]{1,0:T(8,128)(2,1)S(1)}, bf16[128,768]{1,0:T(8,128)(2,1)S(1)}, u32[]{:S(2)}, u32[]{:S(2)}) %collective-permute-start.4) | collective-permute-done | bytes 196640 | tf_op jit(solution)/shard_map/ppermute | solution.py:14
  60.2 0.1 multiply_reduce_fusion.1
  60.3 0.2 add_subtract_fusion.1
  60.5 0.1 copy.39
  60.6 0.1 broadcast_in_dim.13.clone
  60.7 2.6 %sort.258 = (f32[128,128]{0,1:T(8,128)S(1)}, s32[128,128]{0,1:T(8,128)S(1)}, s32[128,128]{0,1:T(8,128)}) sort(f32[128,128]{0,1:T(8,128)S(1)} %copy.39, s32[128,128]{0,1:T(8,128)S(1)} %broadcast_in_dim.13.clone, s32[128,128]{0,1:T(8,128)S(1)} %iota.33.clone), dimensions={1}, to_apply=%region_10.0 | sort | flops 229376 | bytes 393216 | tf_op jit(solution)/shard_map/sort | solution.py:26
  63.3 1.4 %sort.259 = (f32[128,64]{0,1:T(8,128)S(1)}, s32[128,64]{0,1:T(8,128)S(1)}, s32[128,64]{0,1:T(8,128)}) sort(f32[128,64]{0,1:T(8,128)S(1)} %pad_maximum_fusion.3, s32[128,64]{0,1:T(8,128)S(1)} %pad_add_fusion.3, s32[128,64]{0,1:T(8,128)S(1)} %iota.39), dimensions={1}, to_apply=%region_11.0 | sort | flops 106496 | bytes 196608 | tf_op jit(solution)/shard_map/sort | solution.py:26
  64.7 8.8 %collective-permute-done.6 = bf16[128,768]{1,0:T(8,128)(2,1)S(1)} collective-permute-done((bf16[128,768]{1,0:T(8,128)(2,1)S(1)}, bf16[128,768]{1,0:T(8,128)(2,1)S(1)}, u32[]{:S(2)}, u32[]{:S(2)}) %collective-permute-start.6) | collective-permute-done | bytes 196640 | tf_op jit(solution)/shard_map/ppermute | solution.py:14
  73.5 0.1 multiply_reduce_fusion
  73.6 0.2 add_subtract_fusion
  73.8 0.1 copy.45
  73.9 0.1 broadcast_in_dim.14.clone
  74.0 2.6 %sort.260 = (f32[128,128]{0,1:T(8,128)S(1)}, s32[128,128]{0,1:T(8,128)S(1)}, s32[128,128]{0,1:T(8,128)}) sort(f32[128,128]{0,1:T(8,128)S(1)} %copy.45, s32[128,128]{0,1:T(8,128)S(1)} %broadcast_in_dim.14.clone, s32[128,128]{0,1:T(8,128)S(1)} %iota.33.clone), dimensions={1}, to_apply=%region_13.0 | sort | flops 229376 | bytes 393216 | tf_op jit(solution)/shard_map/sort | solution.py:26
  76.6 1.4 %sort.261 = (f32[128,64]{0,1:T(8,128)S(1)}, s32[128,64]{0,1:T(8,128)S(1)}, s32[128,64]{0,1:T(8,128)}) sort(f32[128,64]{0,1:T(8,128)S(1)} %pad_maximum_fusion.4, s32[128,64]{0,1:T(8,128)S(1)} %pad_add_fusion.4, s32[128,64]{0,1:T(8,128)S(1)} %iota.41), dimensions={1}, to_apply=%region_14.0 | sort | flops 106496 | bytes 196608 | tf_op jit(solution)/shard_map/sort | solution.py:26
  78.0 12.2 %all-gather = f32[512,32]{0,1:T(8,128)S(1)} all-gather(f32[128,32]{0,1:T(8,128)S(1)} %slice.88), channel_id=2, replica_groups=mesh['loop'=64,'layer'=4] {'layer'}, dimensions={0}, use_global_device_ids=true | all-gather | bytes 81920 | tf_op jit(solution)/shard_map/all_gather | solution.py:18
  90.2 0.6 copy-done.1
  90.9 5.2 %all-gather.1 = s32[512,32]{0,1:T(8,128)S(1)} all-gather(s32[128,32]{0,1:T(8,128)S(1)} %slice.90), channel_id=3, replica_groups=mesh['loop'=64,'layer'=4] {'layer'}, dimensions={0}, use_global_device_ids=true | all-gather | bytes 81920 | tf_op jit(solution)/shard_map/all_gather | solution.py:18
  96.1 0.6 copy-done.2
  96.7 0.2 slice-done
  96.9 0.8 slice-done.2
  97.7 0.7 slice-done.1
  98.4 0.0 slice-done.3
  98.5 4.5 %while.12 = (s32[]{:T(128)}, f32[128,32]{0,1:T(8,128)S(1)}, s32[128,32]{0,1:T(8,128)S(1)}, f32[3,128,32]{1,0,2:T(4,128)S(1)}, s32[3,128,32]{1,0,2:T(4,128)S(1)}, /*index=5*/s32[]{:T(128)}) while((s32[]{:T(128)}, f32[128,32]{0,1:T(8,128)S(1)}, s32[128,32]{0,1:T(8,128)S(1)}, f32[3,128,32]{1,0,2:T(4,128)S(1)}, s32[3,128,32]{1,0,2:T(4,128)S(1)}, ...), condition=%wide.region_17.18_spmd, body=%wide.region_15.17_spmd.sunk | while | flops 122882 | bytes 491597 | solution.py:21
  98.5 1.4 %sort.264 = (f32[128,64]{0,1:T(8,128)S(1)}, s32[128,64]{0,1:T(8,128)S(1)}, s32[128,64]{0,1:T(8,128)}) sort(f32[128,64]{0,1:T(8,128)S(1)} %pad_maximum_fusion.6, s32[128,64]{0,1:T(8,128)S(1)} %pad_add_fusion.6, s32[128,64]{0,1:T(8,128)S(1)} %iota.44), dimensions={1}, to_apply=%region_16.16 | sort | flops 106496 | bytes 196608 | tf_op jit(solution)/shard_map/while/body/eval_jaxpr/sort | solution.py:26
  100.0 1.4 %sort.264 = (f32[128,64]{0,1:T(8,128)S(1)}, s32[128,64]{0,1:T(8,128)S(1)}, s32[128,64]{0,1:T(8,128)}) sort(f32[128,64]{0,1:T(8,128)S(1)} %pad_maximum_fusion.6, s32[128,64]{0,1:T(8,128)S(1)} %pad_add_fusion.6, s32[128,64]{0,1:T(8,128)S(1)} %iota.44), dimensions={1}, to_apply=%region_16.16 | sort | flops 106496 | bytes 196608 | tf_op jit(solution)/shard_map/while/body/eval_jaxpr/sort | solution.py:26
  101.5 1.4 %sort.264 = (f32[128,64]{0,1:T(8,128)S(1)}, s32[128,64]{0,1:T(8,128)S(1)}, s32[128,64]{0,1:T(8,128)}) sort(f32[128,64]{0,1:T(8,128)S(1)} %pad_maximum_fusion.6, s32[128,64]{0,1:T(8,128)S(1)} %pad_add_fusion.6, s32[128,64]{0,1:T(8,128)S(1)} %iota.44), dimensions={1}, to_apply=%region_16.16 | sort | flops 106496 | bytes 196608 | tf_op jit(solution)/shard_map/while/body/eval_jaxpr/sort | solution.py:26
  102.9 0.1 constant_dynamic-slice_fusion.2
  103.0 0.1 constant_dynamic-slice_fusion.3
  103.1 1.0 sort.262
  104.1 0.7 copy.19
  104.8 0.7 copy.20
  (68 shorter events, 0.4 us)
Async XLA Ops:
  0.6 16.3 %copy-start.3 = (bf16[128,768]{1,0:T(8,128)(2,1)S(1)}, bf16[128,768]{1,0:T(8,128)(2,1)}, u32[]{:S(2)}) copy-start(bf16[128,768]{1,0:T(8,128)(2,1)} %param.6) | copy-start | bytes 589828
  0.6 16.2 %copy-start = (bf16[128,768]{1,0:T(8,128)(2,1)S(1)}, bf16[128,768]{1,0:T(8,128)(2,1)}, u32[]{:S(2)}) copy-start(bf16[128,768]{1,0:T(8,128)(2,1)} %param.5) | copy-start | bytes 589828
  0.6 32.5 %collective-permute-start = (bf16[128,768]{1,0:T(8,128)(2,1)}, bf16[128,768]{1,0:T(8,128)(2,1)S(1)}, u32[]{:S(2)}, u32[]{:S(2)}) collective-permute-start(bf16[128,768]{1,0:T(8,128)(2,1)} %param.6), channel_id=1, source_target_pairs={{0,4},{4,8},{8,12},{12,16},{16,20},{20,24},{24,28},{28,32},{32,36}... | collective-permute-start | bytes 589832 | tf_op jit(solution)/shard_map/ppermute | solution.py:14
  3.2 13.7 %collective-permute-start.1 = (s32[128]{0:T(128)}, s32[128]{0:T(128)S(1)}, u32[]{:S(2)}, u32[]{:S(2)}) collective-permute-start(s32[128]{0:T(128)} %param.7), channel_id=1, source_target_pairs={{0,4},{4,8},{8,12},{12,16},{16,20},{20,24},{24,28},{28,32},{32,36}... | collective-permute-start | bytes 1544 | tf_op jit(solution)/shard_map/ppermute | solution.py:14
  16.9 8.1 %collective-permute-start.3 = (s32[128]{0:T(128)S(1)}, s32[128]{0:T(128)S(1)}, u32[]{:S(2)}, u32[]{:S(2)}) collective-permute-start(s32[128]{0:T(128)S(1)} %collective-permute-done.1), channel_id=1, source_target_pairs={{0,4},{4,8},{8,12},{12,16},{16,20},{20,24},{24,28},{28,32},{32,36}... | collective-permute-start | bytes 1544 | tf_op jit(solution)/shard_map/ppermute | solution.py:14
  17.2 0.7 copy-start.4
  25.0 8.1 %collective-permute-start.5 = (s32[128]{0:T(128)S(1)}, s32[128]{0:T(128)S(1)}, u32[]{:S(2)}, u32[]{:S(2)}) collective-permute-start(s32[128]{0:T(128)S(1)} %collective-permute-done.3), channel_id=1, source_target_pairs={{0,4},{4,8},{8,12},{12,16},{16,20},{20,24},{24,28},{28,32},{32,36}... | collective-permute-start | bytes 1544 | tf_op jit(solution)/shard_map/ppermute | solution.py:14
  33.1 40.8 %collective-permute-start.7 = (s32[128]{0:T(128)S(1)}, s32[128]{0:T(128)S(1)}, u32[]{:S(2)}, u32[]{:S(2)}) collective-permute-start(s32[128]{0:T(128)S(1)} %collective-permute-done.5), channel_id=1, source_target_pairs={{0,4},{4,8},{8,12},{12,16},{16,20},{20,24},{24,28},{28,32},{32,36}... | collective-permute-start | bytes 1544 | tf_op jit(solution)/shard_map/ppermute | solution.py:14
  36.3 10.5 %collective-permute-start.2 = (bf16[128,768]{1,0:T(8,128)(2,1)S(1)}, bf16[128,768]{1,0:T(8,128)(2,1)S(1)}, u32[]{:S(2)}, u32[]{:S(2)}) collective-permute-start(bf16[128,768]{1,0:T(8,128)(2,1)S(1)} %collective-permute-done), channel_id=1, source_target_pairs={{0,4},{4,8},{8,12},{12,16},{16,20},{20,24},{24,28},{28,32},{32,36}... | collective-permute-start | bytes 589832 | tf_op jit(solution)/shard_map/ppermute | solution.py:14
  49.9 10.2 %collective-permute-start.4 = (bf16[128,768]{1,0:T(8,128)(2,1)S(1)}, bf16[128,768]{1,0:T(8,128)(2,1)S(1)}, u32[]{:S(2)}, u32[]{:S(2)}) collective-permute-start(bf16[128,768]{1,0:T(8,128)(2,1)S(1)} %collective-permute-done.2), channel_id=1, source_target_pairs={{0,4},{4,8},{8,12},{12,16},{16,20},{20,24},{24,28},{28,32},{32,36}... | collective-permute-start | bytes 589832 | tf_op jit(solution)/shard_map/ppermute | solution.py:14
  63.2 10.2 %collective-permute-start.6 = (bf16[128,768]{1,0:T(8,128)(2,1)S(1)}, bf16[128,768]{1,0:T(8,128)(2,1)S(1)}, u32[]{:S(2)}, u32[]{:S(2)}) collective-permute-start(bf16[128,768]{1,0:T(8,128)(2,1)S(1)} %collective-permute-done.4), channel_id=1, source_target_pairs={{0,4},{4,8},{8,12},{12,16},{16,20},{20,24},{24,28},{28,32},{32,36}... | collective-permute-start | bytes 589832 | tf_op jit(solution)/shard_map/ppermute | solution.py:14
  90.2 0.6 copy-start.1
  96.1 0.6 copy-start.2
  96.1 0.8 slice-start
  96.9 0.8 slice-start.2
  97.7 0.7 slice-start.1
  97.7 0.7 slice-start.3
where the time goes:
time: 106 us; the launch traced here: 105 us
  waiting for transfers between devices  49.2 us (46%)
  other arithmetic  25.6 us (24%)
  blocking collectives  17.4 us (16%)
  local copies, waits for them, and re-layouts  6.65 us (6%)
  starting transfers between devices  4.46 us (4%)
  matrix products  1.07 us (1%)
    ppermute x8, waiting for transfers between devices, from_behind(): return lax.ppermute(value, axis, pairs)  49.2 us
    sort x12, other arithmetic, select(): ordered = lax.sort((dist, ids), dimension=1, num_keys=2)  22.7 us
    all_gather x2, blocking collectives, combined_all(): pieces = jax.tree.map(lambda part: lax.all_gather(part, axis), value)  17.4 us
    ppermute x8, starting transfers between devices, from_behind(): return lax.ppermute(value, axis, pairs)  4.46 us
    unnamed x17, local copies, waits for them, and re-layouts  3.68 us
  transfers between devices with their start and end apart: 8, of which 6 were waited for; matrix products, arithmetic and copies ran while one was open for 18% of the time, Pallas kernels for 0%

commit v1 on v0

v1 whole, which is shorter than its diff:
```python
import jax
import jax.numpy as jnp
from jax import lax
from jax.experimental import pallas as pl
from jax.experimental.pallas import tpu as pltpu
from jax.sharding import PartitionSpec as P

D = 768
K = 32
STEPS = 4
LOOP = 64
ROW = 8
LAYERS = 4
CB = 128
ROWS = 32
RELAY = 5
CHUNKS = 2
PIECE = ROWS // CHUNKS
CAND_CHUNKS = 2
CAND_PIECE = CB // CAND_CHUNKS
MESH = pl.DeviceIdType.MESH
NT = (((1,), (1,)), ((), ()))


def batcher(count):
    pairs = []
    p = 1
    while p < count:
        k = p
        while k >= 1:
            for j in range(k % p, count - k, 2 * k):
                for i in range(min(k, count - j - k)):
                    if (i + j) // (2 * p) == (i + j + k) // (2 * p):
                        pairs.append((i + j, i + j + k))
            k //= 2
        p *= 2
    return pairs


SORT16 = batcher(16)


def exchange(values, low, high):
    a, b = values[low], values[high]
    values[low], values[high] = jnp.minimum(a, b), jnp.maximum(a, b)


def settle(values):
    for gap in (8, 4, 2, 1):
        for k in range(16):
            if not k & gap:
                exchange(values, k, k + gap)


def smallest(key):
    row = lax.broadcasted_iota(jnp.int32, (8, 128), 0)
    upper = row >= 4
    v = [key[8 * g : 8 * g + 8, :] for g in range(16)]
    for low, high in SORT16:
        exchange(v, low, high)
    r = [pltpu.roll(v[15 - k], 4, 0) for k in range(16)]
    v = [jnp.where(upper, jnp.maximum(v[k], r[k]), jnp.minimum(v[k], r[k])) for k in range(16)]
    settle(v)
    for shift, lanes in ((2, 0), (3, 0), (4, 96), (4, 64)):
        r = [pltpu.roll(v[15 - k], shift, 0) for k in range(16)]
        if lanes:
            r = [pltpu.roll(x, lanes, 1) for x in r]
        v = [jnp.minimum(v[k], r[k]) for k in range(16)]
        r = [pltpu.roll(x, 4, 0) for x in v]
        v = [jnp.where(upper, jnp.maximum(v[k], r[k]), jnp.minimum(v[k], r[k])) for k in range(16)]
        settle(v)
    return v


def by_layer(parts):
    group = lax.broadcasted_iota(jnp.int32, parts[0].shape, 1) // ROWS
    return jnp.where(
        group < 2, jnp.where(group == 0, parts[0], parts[1]), jnp.where(group == 2, parts[2], parts[3])
    )


def merged(first, second):
    place = lax.broadcasted_iota(jnp.int32, (K, 128), 0)

    def before(a, b):
        return (a[0] < b[0]) | ((a[0] == b[0]) & (a[1] < b[1]))

    lower = before(first, second)
    now = [jnp.where(lower, a, b) for a, b in zip(first, second)]
    for gap in (16, 8, 4, 2, 1):
        head = (place & gap) == 0
        other = [jnp.where(head, pltpu.roll(x, K - gap, 0), pltpu.roll(x, gap, 0)) for x in now]
        keep = before(now, other) == head
        now = [jnp.where(keep, a, b) for a, b in zip(now, other)]
    return now


def kernel(
    q_ref, c_ref, id_ref, dist_ref, near_ref,
    slots, cands, idents, base, table, keys, mine, outbox, inbox,
    local_sem, slot_send, slot_recv, relay_send, cand_send, cand_recv, id_send, id_recv, res_send, res_recv, ring_sem,
):
    i, l = lax.axis_index("loop"), lax.axis_index("layer")
    z = lax.rem(i, ROW)

    def at(offset):
        return (lax.rem(i + offset + 2 * LOOP, LOOP), l)

    def remote(src, dst, send, recv, device):
        return pltpu.make_async_remote_copy(
            src_ref=src, dst_ref=dst, send_sem=send, recv_sem=recv, device_id=device, device_id_type=MESH
        )

    own_q = pltpu.make_async_copy(q_ref.at[pl.ds(l * ROWS, ROWS)], slots.at[0], local_sem.at[0])
    own_c = pltpu.make_async_copy(c_ref, cands.at[l], local_sem.at[1])
    own_id = pltpu.make_async_copy(id_ref, idents.at[l], local_sem.at[2])
    own_q.start()
    own_id.start()
    own_c.start()

    barrier = pltpu.get_barrier_semaphore()

    def hello(device):
        pl.semaphore_signal(barrier, inc=1, device_id=device, device_id_type=MESH)

    @pl.when(z == 0)
    def _():
        for k in range(4):
            hello(at(ROW + k))
        hello(at(ROW - 1))

    @pl.when(z < ROW - 1)
    def _():
        hello(at(1))

    for k in (1, 2, 3):
        hello((i, l ^ k))
    own_q.wait()
    own_id.wait()
    own_c.wait()
    extra = jnp.where((z >= 1) & (z <= 3), 1, 0) + jnp.where(z == ROW - 1, 1, 0)
    pl.semaphore_wait(barrier, 4 + extra)

    first = jnp.where(z == 0, RELAY, 0)
    below = at(jnp.where(z == 0, ROW - 1, -1))

    def slot_copy(source, target, chunk, device):
        rows = pl.ds(chunk * PIECE, PIECE)
        return remote(
            slots.at[source, rows], slots.at[target, rows],
            slot_send.at[target, chunk], slot_recv.at[target, chunk], device,
        )

    def relay_copy(chunk):
        rows = pl.ds(chunk * PIECE, PIECE)
        return remote(
            slots.at[0, rows], slots.at[RELAY + z, rows],
            relay_send.at[chunk], slot_recv.at[RELAY + z, chunk], at(-z - ROW),
        )

    def arrived(slot, chunk):
        rows = pl.ds(chunk * PIECE, PIECE)
        remote(
            slots.at[0, rows], slots.at[slot, rows], slot_send.at[1, chunk], slot_recv.at[slot, chunk], below
        ).wait_recv()

    def pass_on(s, chunk):
        slot_copy(first + s, s + 1, chunk, below).start()

    @pl.when(z < 4)
    def _():
        for chunk in range(CHUNKS):
            relay_copy(chunk).start()

    @pl.when(z == ROW - 1)
    def _():
        pl.semaphore_signal(ring_sem, inc=1, device_id=at(1 - ROW), device_id_type=MESH)

    @pl.when(z > 0)
    def _():
        for chunk in range(CHUNKS):
            pass_on(0, chunk)

    def cand_copy(block, chunk, kind, device):
        rows = pl.ds(chunk * CAND_PIECE, CAND_PIECE)
        return remote(
            cands.at[block, rows], cands.at[block, rows],
            cand_send.at[kind, chunk], cand_recv.at[kind, chunk], device,
        )

    def id_copy(k, block):
        return remote(
            idents.at[block], idents.at[block], id_send.at[k - 1], id_recv.at[k - 1], (i, l ^ k)
        )

    for k in (1, 2, 3):
        id_copy(k, l).start()
    for chunk in range(CAND_CHUNKS):
        cand_copy(l, chunk, 1, (i, l ^ 2)).start()
    for chunk in range(CAND_CHUNKS):
        cand_copy(l, chunk, 0, (i, l ^ 1)).start()

    for k in (1, 2, 3):
        id_copy(k, l ^ k).wait_recv()
    lane = lax.broadcasted_iota(jnp.int32, (CB, 128), 1)
    id_rows = [idents[m].astype(jnp.float32) for m in range(LAYERS)]
    id_cols = jnp.concatenate([jnp.broadcast_to(x, (ROWS, CB)) for x in id_rows], 0).T
    part = jnp.zeros((CB, 128), jnp.float32)
    for m in range(LAYERS):
        for k in range(4):
            shifted = pltpu.roll(jnp.broadcast_to(id_rows[m], (8, 128)), 32 * k, 1)[:1]
            part += jnp.where(shifted < id_cols, 1.0, 0.0)
    same = lax.broadcasted_iota(jnp.int32, (128, 128), 0) // ROWS == (
        lax.broadcasted_iota(jnp.int32, (128, 128), 1) // ROWS
    )
    rank = jnp.dot(
        part.astype(jnp.bfloat16),
        jnp.where(same, 1.0, 0.0).astype(jnp.bfloat16),
        preferred_element_type=jnp.float32,
    ).astype(jnp.int32)
    for a in range(4):
        total = jnp.zeros((1, 128), jnp.float32)
        for m in range(LAYERS):
            column = rank[:, ROWS * m : ROWS * m + 1]
            ident = id_cols[:, ROWS * m : ROWS * m + 1]
            total += jnp.sum(jnp.where(column == lane + 128 * a, ident, 0.0), 0, keepdims=True)
        table[a] = jnp.broadcast_to(total, (8, 128)).astype(jnp.int32)

    def cand_forward(chunk):
        cand_copy(l ^ 2, chunk, 1, (i, l ^ 2)).wait_recv()
        cand_copy(l ^ 2, chunk, 2, (i, l ^ 1)).start()

    @pl.when(z == 0)
    def _():
        for chunk in range(CAND_CHUNKS):
            cand_forward(chunk)
        pl.semaphore_wait(ring_sem, 1)
        for s in range(4):
            for chunk in range(CHUNKS):
                arrived(RELAY + s, chunk)
                pass_on(s, chunk)

    @pl.when(z > 0)
    def _():
        for s in (1, 2, 3):
            for chunk in range(CHUNKS):
                arrived(s, chunk)
                pass_on(s, chunk)
            if s <= CAND_CHUNKS:
                cand_forward(s - 1)

    for chunk in range(CAND_CHUNKS):
        cand_copy(l ^ 1, chunk, 0, (i, l ^ 1)).wait_recv()
    for chunk in range(CAND_CHUNKS):
        cand_copy(l ^ 3, chunk, 2, (i, l ^ 1)).wait_recv()

    ones = jnp.ones((128, D), jnp.bfloat16)
    norms = []
    for m in range(LAYERS):
        block = cands[m]
        norms.append(lax.dot_general(block * block, ones, NT, preferred_element_type=jnp.float32))
    base[...] = by_layer(norms).astype(jnp.int32) * 512 + rank

    start = jnp.where(z >= 4, ROW - z, 1)

    def result_copy(s):
        return remote(
            outbox.at[s], inbox.at[s - 1], res_send.at[s - 1], res_recv.at[s - 1], at(s)
        )

    def step(t, carry):
        s = lax.rem(start + t, STEPS + 1)

        @pl.when((s == 4) | ((z == 0) & (s > 0)))
        def _():
            for chunk in range(CHUNKS):
                arrived(s, chunk)

        block = slots[s]
        four = jnp.concatenate([block] * 4, 0)
        inner = by_layer(
            [lax.dot_general(cands[m], four, NT, preferred_element_type=jnp.float32) for m in range(LAYERS)]
        )
        v = smallest(base[...] - inner.astype(jnp.int32) * 1024)

        @pl.when(s == 0)
        def _():
            for k in range(16):
                keys[k : k + 1, :] = v[k][0:1, :]
                keys[16 + k : 17 + k, :] = v[k][4:5, :]

        @pl.when(s > 0)
        def _():
            for k in range(16):
                keys[31 - k : 32 - k, :] = v[k][0:1, :]
                keys[15 - k : 16 - k, :] = v[k][4:5, :]

        left = lax.broadcasted_iota(jnp.int32, (8, 128), 1) < ROWS
        for g in range(4):
            key = keys[8 * g : 8 * g + 8, :]
            place = key & 127
            which = (key >> 7) & 3
            found = [jnp.take_along_axis(table[a], place, axis=1, mode="promise_in_bounds") for a in range(4)]
            ident = jnp.where(
                which < 2, jnp.where(which == 0, found[0], found[1]), jnp.where(which == 2, found[2], found[3])
            )
            outbox[s, 8 * g : 8 * g + 8, :] = jnp.where(left, key >> 9, pltpu.roll(ident, ROWS, 1))

        @pl.when(s > 0)
        def _():
            result_copy(s).start()

        return carry

    lax.fori_loop(0, STEPS + 1, step, 0)

    def pair(x):
        return [x, pltpu.roll(x, 128 - ROWS, 1)]

    best = pair(outbox[0])
    for s in range(1, STEPS + 1):
        result_copy(s).wait_recv()
        best = merged(best, pair(inbox[s - 1]))
    block = slots[0]
    own = lax.dot_general(ones, jnp.concatenate([block * block] * 4, 0), NT, preferred_element_type=jnp.float32)
    dist = (best[0].astype(jnp.float32) + own[:K, :]) * (0.125 / D)
    both = jnp.concatenate([dist, best[1].astype(jnp.float32), dist, dist], 0).T
    dist_ref[...] = both[:ROWS, :K]
    near_ref[...] = both[:ROWS, K : 2 * K].astype(jnp.int32)

    for s in range(1, STEPS + 1):
        result_copy(s).wait_send()
        for chunk in range(CHUNKS):
            slot_copy(0, s, chunk, below).wait_send()
    for k in (1, 2, 3):
        id_copy(k, l).wait_send()
    for chunk in range(CAND_CHUNKS):
        for kind in range(3):
            cand_copy(l, chunk, kind, (i, l ^ 1)).wait_send()

    @pl.when(z < 4)
    def _():
        for chunk in range(CHUNKS):
            relay_copy(chunk).wait_send()


def shards(queries, candidates, cand_ids):
    dma = pltpu.SemaphoreType.DMA
    any_space = pl.BlockSpec(memory_space=pltpu.HBM)
    vmem = pl.BlockSpec(memory_space=pltpu.VMEM)
    return pl.pallas_call(
        kernel,
        out_shape=(
            jax.ShapeDtypeStruct((ROWS, K), jnp.float32),
            jax.ShapeDtypeStruct((ROWS, K), jnp.int32),
        ),
        in_specs=[any_space, any_space, any_space],
        out_specs=(vmem, vmem),
        scratch_shapes=[
            pltpu.VMEM((RELAY + 4, ROWS, D), jnp.bfloat16),
            pltpu.VMEM((LAYERS, CB, D), jnp.bfloat16),
            pltpu.VMEM((LAYERS, 1, CB), jnp.int32),
            pltpu.VMEM((CB, 128), jnp.int32),
            pltpu.VMEM((4, 8, 128), jnp.int32),
            pltpu.VMEM((K, 128), jnp.int32),
            pltpu.VMEM((K, 128), jnp.int32),
            pltpu.VMEM((STEPS + 1, K, 128), jnp.int32),
            pltpu.VMEM((STEPS, K, 128), jnp.int32),
            dma((3,)),
            dma((STEPS + 1, CHUNKS)),
            dma((RELAY + 4, CHUNKS)),
            dma((CHUNKS,)),
            dma((3, CAND_CHUNKS)),
            dma((3, CAND_CHUNKS)),
            dma((3,)),
            dma((3,)),
            dma((STEPS,)),
            dma((STEPS,)),
            pltpu.SemaphoreType.REGULAR,
        ],
        compiler_params=pltpu.CompilerParams(
            collective_id=0, has_side_effects=True, vmem_limit_bytes=16 * 1024 * 1024
        ),
    )(queries, candidates, cand_ids.reshape(1, CB))


def solution(mesh):
    return jax.shard_map(
        shards,
        mesh=mesh,
        in_specs=(P("loop", None), P(("loop", "layer"), None), P(("loop", "layer"))),
        out_specs=(P(("loop", "layer"), None), P(("loop", "layer"), None)),
        check_vma=False,
    )
```

time: 106 us -> 39.6 us (0.37)
  the two profiles are of different devices: /device:TPU:1 before, /device:TPU:6 now
where the time goes in v1:
time: 39.6 us; the launch traced here: 39.5 us
  Pallas kernels  35.1 us (89%)
  local copies, waits for them, and re-layouts  3.71 us (9%)
  between operations  0.65 us (2%)
    pallas_call x1, Pallas kernels, shards(): pl.pallas_call(kernel, out_shape=(jax.ShapeDtypeStruct((ROWS, K), jnp.flo...  35.1 us
    unnamed x8, local copies, waits for them, and re-layouts  3.71 us

profile of v1, /device:TPU:6, one launch (start us, length us, event | category | flops | bytes accessed | tf_op | source)
XLA Modules:
  0.0 39.5 jit_solution(8436288249542116721)
XLA Ops:
  0.6 0.0 copy-start.2
  0.6 0.6 %copy-done.2 = s32[128]{0:T(128)S(1)} copy-done((s32[128]{0:T(128)S(1)}, s32[128]{0:T(128)}, u32[]{:S(2)}) %copy-start.2) | copy-done | bytes 536
  1.3 0.0 copy-start
  1.3 0.9 %copy-done = bf16[128,768]{1,0:T(8,128)(2,1)S(1)} copy-done((bf16[128,768]{1,0:T(8,128)(2,1)S(1)}, bf16[128,768]{1,0:T(8,128)(2,1)}, u32[]{:S(2)}) %copy-start) | copy-done | bytes 196632
  2.2 0.0 copy-start.1
  2.2 0.9 %copy-done.1 = bf16[128,768]{1,0:T(8,128)(2,1)S(1)} copy-done((bf16[128,768]{1,0:T(8,128)(2,1)S(1)}, bf16[128,768]{1,0:T(8,128)(2,1)}, u32[]{:S(2)}) %copy-start.1) | copy-done | bytes 196632
  3.1 35.1 %shard_map.50 = (f32[32,32]{1,0:T(8,128)S(1)}, s32[32,32]{1,0:T(8,128)S(1)}) custom-call(bf16[128,768]{1,0:T(8,128)(2,1)S(1)} %copy-done, bf16[128,768]{1,0:T(8,128)(2,1)S(1)} %copy-done.1, s32[1,128]{1,0:T(1,128)S(1)} %bitcast.1), custom_call_target="tpu_custom_call" | custom-call | tf_op jit(solution)/shard_map/pallas_call | solution.py:351
  38.2 0.6 %copy.7 = f32[32,32]{1,0:T(8,128)} copy(f32[32,32]{1,0:T(8,128)S(1)} %get-tuple-element.4) | data formatting | bytes 8192
  38.9 0.6 %copy.8 = s32[32,32]{1,0:T(8,128)} copy(s32[32,32]{1,0:T(8,128)S(1)} %get-tuple-element.5) | data formatting | bytes 8192
Async XLA Ops:
  0.6 0.7 %copy-start.2 = (s32[128]{0:T(128)S(1)}, s32[128]{0:T(128)}, u32[]{:S(2)}) copy-start(s32[128]{0:T(128)} %param.5) | copy-start | bytes 1540
  1.3 0.9 %copy-start = (bf16[128,768]{1,0:T(8,128)(2,1)S(1)}, bf16[128,768]{1,0:T(8,128)(2,1)}, u32[]{:S(2)}) copy-start(bf16[128,768]{1,0:T(8,128)(2,1)} %q_ref.1) | copy-start | bytes 589828
  2.2 0.9 %copy-start.1 = (bf16[128,768]{1,0:T(8,128)(2,1)S(1)}, bf16[128,768]{1,0:T(8,128)(2,1)}, u32[]{:S(2)}) copy-start(bf16[128,768]{1,0:T(8,128)(2,1)} %c_ref.1) | copy-start | bytes 589828

commit v2 on v1

--- a/solution.py
+++ b/solution.py
@@ -13,10 +13,8 @@
 LAYERS = 4
 CB = 128
 ROWS = 32
-RELAY = 5
-CHUNKS = 2
-PIECE = ROWS // CHUNKS
-CAND_CHUNKS = 2
+PARKED = 5
+CAND_CHUNKS = 4
 CAND_PIECE = CB // CAND_CHUNKS
 MESH = pl.DeviceIdType.MESH
 NT = (((1,), (1,)), ((), ()))
@@ -97,11 +95,13 @@
 
 def kernel(
     q_ref, c_ref, id_ref, dist_ref, near_ref,
-    slots, cands, idents, base, table, keys, mine, outbox, inbox,
-    local_sem, slot_send, slot_recv, relay_send, cand_send, cand_recv, id_send, id_recv, res_send, res_recv, ring_sem,
+    slots, cands, idents, base, table, keys, outbox, inbox,
+    local_sem, chain_send, slot_recv, park_send, spread_send, cand_send, cand_recv, id_send, id_recv,
+    res_send, res_recv, ring_sem,
 ):
     i, l = lax.axis_index("loop"), lax.axis_index("layer")
     z = lax.rem(i, ROW)
+    early = z < 4
 
     def at(offset):
         return (lax.rem(i + offset + 2 * LOOP, LOOP), l)
@@ -114,78 +114,75 @@
     own_q = pltpu.make_async_copy(q_ref.at[pl.ds(l * ROWS, ROWS)], slots.at[0], local_sem.at[0])
     own_c = pltpu.make_async_copy(c_ref, cands.at[l], local_sem.at[1])
     own_id = pltpu.make_async_copy(id_ref, idents.at[l], local_sem.at[2])
+
+    barrier = pltpu.get_barrier_semaphore()
+
+    def hello(device):
+        pl.semaphore_signal(barrier, inc=1, device_id=device, device_id_type=MESH)
+
+    @pl.when(early)
+    def _():
+        hello(at(ROW))
+
+    @pl.when(z < ROW - 1)
+    def _():
+        hello(at(1))
+
+    for offset in (4, 5, 6, 7):
+
+        @pl.when(z + offset < ROW)
+        def _():
+            hello(at(offset))
+
+    for k in (1, 2, 3):
+        hello((i, l ^ k))
     own_q.start()
     own_id.start()
     own_c.start()
-
-    barrier = pltpu.get_barrier_semaphore()
-
-    def hello(device):
-        pl.semaphore_signal(barrier, inc=1, device_id=device, device_id_type=MESH)
-
-    @pl.when(z == 0)
-    def _():
-        for k in range(4):
-            hello(at(ROW + k))
-        hello(at(ROW - 1))
-
-    @pl.when(z < ROW - 1)
-    def _():
-        hello(at(1))
-
-    for k in (1, 2, 3):
-        hello((i, l ^ k))
     own_q.wait()
     own_id.wait()
-    own_c.wait()
-    extra = jnp.where((z >= 1) & (z <= 3), 1, 0) + jnp.where(z == ROW - 1, 1, 0)
-    pl.semaphore_wait(barrier, 4 + extra)
-
-    first = jnp.where(z == 0, RELAY, 0)
-    below = at(jnp.where(z == 0, ROW - 1, -1))
-
-    def slot_copy(source, target, chunk, device):
-        rows = pl.ds(chunk * PIECE, PIECE)
+    pl.semaphore_wait(barrier, jnp.where(early, 4 + jnp.where(z > 0, 1, 0), z + 1))
+
+    def park_copy():
+        return remote(slots.at[0], slots.at[PARKED], park_send, slot_recv.at[PARKED], at(-ROW))
+
+    def chain_copy(s):
+        return remote(slots.at[s], slots.at[s + 1], chain_send.at[s], slot_recv.at[s + 1], at(-1))
+
+    def spread_copy(s):
+        return remote(slots.at[PARKED], slots.at[s], spread_send.at[s - 1], slot_recv.at[s], at(ROW - s))
+
+    def arrived(slot):
+        remote(slots.at[0], slots.at[slot], park_send, slot_recv.at[slot], at(1)).wait_recv()
+
+    for e in range(4):
+
+        @pl.when(z >= 4 + e)
+        def _():
+            pl.semaphore_signal(ring_sem, inc=1, device_id=at(e - z), device_id_type=MESH)
+
+    @pl.when(early)
+    def _():
+        park_copy().start()
+
+    @pl.when(z > 0)
+    def _():
+        chain_copy(0).start()
+
+    def across_copy(chunk, block):
+        rows = pl.ds(chunk * CAND_PIECE, CAND_PIECE)
         return remote(
-            slots.at[source, rows], slots.at[target, rows],
-            slot_send.at[target, chunk], slot_recv.at[target, chunk], device,
-        )
-
-    def relay_copy(chunk):
-        rows = pl.ds(chunk * PIECE, PIECE)
-        return remote(
-            slots.at[0, rows], slots.at[RELAY + z, rows],
-            relay_send.at[chunk], slot_recv.at[RELAY + z, chunk], at(-z - ROW),
-        )
-
-    def arrived(slot, chunk):
-        rows = pl.ds(chunk * PIECE, PIECE)
-        remote(
-            slots.at[0, rows], slots.at[slot, rows], slot_send.at[1, chunk], slot_recv.at[slot, chunk], below
-        ).wait_recv()
-
-    def pass_on(s, chunk):
-        slot_copy(first + s, s + 1, chunk, below).start()
-
-    @pl.when(z < 4)
-    def _():
-        for chunk in range(CHUNKS):
-            relay_copy(chunk).start()
-
-    @pl.when(z == ROW - 1)
-    def _():
-        pl.semaphore_signal(ring_sem, inc=1, device_id=at(1 - ROW), device_id_type=MESH)
-
-    @pl.when(z > 0)
-    def _():
-        for chunk in range(CHUNKS):
-            pass_on(0, chunk)
-
-    def cand_copy(block, chunk, kind, device):
+            c_ref.at[rows], cands.at[block, rows], cand_send.at[0, chunk], cand_recv.at[0, chunk], (i, l ^ 2)
+        )
+
+    def beside_copy(block):
+        return remote(c_ref, cands.at[block], cand_send.at[1, 0], cand_recv.at[1, 0], (i, l ^ 1))
+
+    def onward_copy(chunk, block):
         rows = pl.ds(chunk * CAND_PIECE, CAND_PIECE)
         return remote(
             cands.at[block, rows], cands.at[block, rows],
-            cand_send.at[kind, chunk], cand_recv.at[kind, chunk], device,
+            cand_send.at[2, chunk], cand_recv.at[2, chunk], (i, l ^ 1),
         )
 
     def id_copy(k, block):
@@ -193,12 +190,11 @@
             idents.at[block], idents.at[block], id_send.at[k - 1], id_recv.at[k - 1], (i, l ^ k)
         )
 
+    for chunk in range(CAND_CHUNKS):
+        across_copy(chunk, l).start()
     for k in (1, 2, 3):
         id_copy(k, l).start()
-    for chunk in range(CAND_CHUNKS):
-        cand_copy(l, chunk, 1, (i, l ^ 2)).start()
-    for chunk in range(CAND_CHUNKS):
-        cand_copy(l, chunk, 0, (i, l ^ 1)).start()
+    beside_copy(l).start()
 
     for k in (1, 2, 3):
         id_copy(k, l ^ k).wait_recv()
@@ -226,33 +222,28 @@
             total += jnp.sum(jnp.where(column == lane + 128 * a, ident, 0.0), 0, keepdims=True)
         table[a] = jnp.broadcast_to(total, (8, 128)).astype(jnp.int32)
 
-    def cand_forward(chunk):
-        cand_copy(l ^ 2, chunk, 1, (i, l ^ 2)).wait_recv()
-        cand_copy(l ^ 2, chunk, 2, (i, l ^ 1)).start()
-
-    @pl.when(z == 0)
-    def _():
-        for chunk in range(CAND_CHUNKS):
-            cand_forward(chunk)
-        pl.semaphore_wait(ring_sem, 1)
-        for s in range(4):
-            for chunk in range(CHUNKS):
-                arrived(RELAY + s, chunk)
-                pass_on(s, chunk)
-
-    @pl.when(z > 0)
-    def _():
-        for s in (1, 2, 3):
-            for chunk in range(CHUNKS):
-                arrived(s, chunk)
-                pass_on(s, chunk)
-            if s <= CAND_CHUNKS:
-                cand_forward(s - 1)
+    @pl.when((z > 0) & (z < ROW - 1))
+    def _():
+        arrived(1)
+        chain_copy(1).start()
+
+    @pl.when(early)
+    def _():
+        arrived(PARKED)
+        pl.semaphore_wait(ring_sem, 4 - z)
+        for s in (4, 3, 2, 1):
+
+            @pl.when(s > z)
+            def _():
+                spread_copy(s).start()
 
     for chunk in range(CAND_CHUNKS):
-        cand_copy(l ^ 1, chunk, 0, (i, l ^ 1)).wait_recv()
+        across_copy(chunk, l ^ 2).wait_recv()
+        onward_copy(chunk, l ^ 2).start()
+    own_c.wait()
+    beside_copy(l ^ 1).wait_recv()
     for chunk in range(CAND_CHUNKS):
-        cand_copy(l ^ 3, chunk, 2, (i, l ^ 1)).wait_recv()
+        onward_copy(chunk, l ^ 3).wait_recv()
 
     ones = jnp.ones((128, D), jnp.bfloat16)
     norms = []
@@ -261,20 +252,25 @@
         norms.append(lax.dot_general(block * block, ones, NT, preferred_element_type=jnp.float32))
     base[...] = by_layer(norms).astype(jnp.int32) * 512 + rank
 
-    start = jnp.where(z >= 4, ROW - z, 1)
-
     def result_copy(s):
         return remote(
             outbox.at[s], inbox.at[s - 1], res_send.at[s - 1], res_recv.at[s - 1], at(s)
         )
 
     def step(t, carry):
-        s = lax.rem(start + t, STEPS + 1)
-
-        @pl.when((s == 4) | ((z == 0) & (s > 0)))
-        def _():
-            for chunk in range(CHUNKS):
-                arrived(s, chunk)
+        s = jnp.where(
+            (z == 4) & (t >= 2),
+            jnp.where(t == 2, 4, t - 1),
+            jnp.where((z == 5) & ((t == 2) | (t == 3)), 5 - t, t),
+        )
+
+        @pl.when((s >= 2) | ((s == 1) & ((z == 0) | (z == ROW - 1))))
+        def _():
+            arrived(s)
+
+        @pl.when((z > 0) & (s >= 2) & (s <= 3) & (s + z < ROW))
+        def _():
+            chain_copy(s).start()
 
         block = slots[s]
         four = jnp.concatenate([block] * 4, 0)
@@ -330,18 +326,25 @@
 
     for s in range(1, STEPS + 1):
         result_copy(s).wait_send()
-        for chunk in range(CHUNKS):
-            slot_copy(0, s, chunk, below).wait_send()
+
+        @pl.when((z > 0) & (s - 1 + z < ROW))
+        def _():
+            chain_copy(s - 1).wait_send()
+
+        @pl.when(early & (s > z))
+        def _():
+            spread_copy(s).wait_send()
+
     for k in (1, 2, 3):
         id_copy(k, l).wait_send()
+    beside_copy(l).wait_send()
     for chunk in range(CAND_CHUNKS):
-        for kind in range(3):
-            cand_copy(l, chunk, kind, (i, l ^ 1)).wait_send()
-
-    @pl.when(z < 4)
-    def _():
-        for chunk in range(CHUNKS):
-            relay_copy(chunk).wait_send()
+        across_copy(chunk, l).wait_send()
+        onward_copy(chunk, l).wait_send()
+
+    @pl.when(early)
+    def _():
+        park_copy().wait_send()
 
 
 def shards(queries, candidates, cand_ids):
@@ -357,19 +360,19 @@
         in_specs=[any_space, any_space, any_space],
         out_specs=(vmem, vmem),
         scratch_shapes=[
-            pltpu.VMEM((RELAY + 4, ROWS, D), jnp.bfloat16),
+            pltpu.VMEM((PARKED + 1, ROWS, D), jnp.bfloat16),
             pltpu.VMEM((LAYERS, CB, D), jnp.bfloat16),
             pltpu.VMEM((LAYERS, 1, CB), jnp.int32),
             pltpu.VMEM((CB, 128), jnp.int32),
             pltpu.VMEM((4, 8, 128), jnp.int32),
             pltpu.VMEM((K, 128), jnp.int32),
-            pltpu.VMEM((K, 128), jnp.int32),
             pltpu.VMEM((STEPS + 1, K, 128), jnp.int32),
             pltpu.VMEM((STEPS, K, 128), jnp.int32),
             dma((3,)),
-            dma((STEPS + 1, CHUNKS)),
-            dma((RELAY + 4, CHUNKS)),
-            dma((CHUNKS,)),
+            dma((STEPS,)),
+            dma((PARKED + 1,)),
+            dma,
+            dma((STEPS,)),
             dma((3, CAND_CHUNKS)),
             dma((3, CAND_CHUNKS)),
             dma((3,)),
@@ -381,7 +384,7 @@
         compiler_params=pltpu.CompilerParams(
             collective_id=0, has_side_effects=True, vmem_limit_bytes=16 * 1024 * 1024
         ),
-    )(queries, candidates, cand_ids.reshape(1, CB))
+    )(*(pltpu.with_memory_space_constraint(x, pltpu.HBM) for x in (queries, candidates, cand_ids.reshape(1, CB))))
 
 
 def solution(mesh):

time: 39.6 us -> 33.1 us (0.84)
  the two profiles are of different devices: /device:TPU:6 before, /device:TPU:64 now
where the time goes in v2:
time: 33.1 us; the launch traced here: 33 us
  Pallas kernels  31.1 us (94%)
  local copies, waits for them, and re-layouts  1.21 us (4%)
  between operations  0.64 us (2%)
    pallas_call x1, Pallas kernels, shards(): pl.pallas_call(kernel, out_shape=(jax.ShapeDtypeStruct((ROWS, K), jnp.flo...  31.1 us
    unnamed x2, local copies, waits for them, and re-layouts  1.21 us

profile of v2, /device:TPU:64, one launch (start us, length us, event | category | flops | bytes accessed | tf_op | source)
XLA Modules:
  0.0 33.0 jit_solution(10780276108520641548)
XLA Ops:
  0.6 31.1 %shard_map.50 = (f32[32,32]{1,0:T(8,128)S(1)}, s32[32,32]{1,0:T(8,128)S(1)}) custom-call(bf16[128,768]{1,0:T(8,128)(2,1)} %q_ref.1, bf16[128,768]{1,0:T(8,128)(2,1)} %c_ref.1, s32[1,128]{1,0:T(1,128)} %bitcast.1), custom_call_target="tpu_custom_call" | custom-call | tf_op jit(solution)/shard_map/pallas_call | solution.py:354
  31.7 0.6 %copy.7 = f32[32,32]{1,0:T(8,128)} copy(f32[32,32]{1,0:T(8,128)S(1)} %get-tuple-element.4) | data formatting | bytes 8192
  32.4 0.6 %copy.8 = s32[32,32]{1,0:T(8,128)} copy(s32[32,32]{1,0:T(8,128)S(1)} %get-tuple-element.5) | data formatting | bytes 8192

commit v3 on v2

--- a/solution.py
+++ b/solution.py
@@ -14,7 +14,7 @@
 CB = 128
 ROWS = 32
 PARKED = 5
-CAND_CHUNKS = 4
+CAND_CHUNKS = 8
 CAND_PIECE = CB // CAND_CHUNKS
 MESH = pl.DeviceIdType.MESH
 NT = (((1,), (1,)), ((), ()))
@@ -97,21 +97,25 @@
     q_ref, c_ref, id_ref, dist_ref, near_ref,
     slots, cands, idents, base, table, keys, outbox, inbox,
     local_sem, chain_send, slot_recv, park_send, spread_send, cand_send, cand_recv, id_send, id_recv,
-    res_send, res_recv, ring_sem,
+    res_send, res_recv, ring_sem, go_sem,
 ):
     i, l = lax.axis_index("loop"), lax.axis_index("layer")
     z = lax.rem(i, ROW)
     early = z < 4
-
-    def at(offset):
-        return (lax.rem(i + offset + 2 * LOOP, LOOP), l)
+    skew = (z == 1) | (z == 2)
+
+    def at(offset, layer=l):
+        return (lax.rem(i + offset + 2 * LOOP, LOOP), layer)
+
+    over = l ^ 2
 
     def remote(src, dst, send, recv, device):
         return pltpu.make_async_remote_copy(
             src_ref=src, dst_ref=dst, send_sem=send, recv_sem=recv, device_id=device, device_id_type=MESH
         )
 
-    own_q = pltpu.make_async_copy(q_ref.at[pl.ds(l * ROWS, ROWS)], slots.at[0], local_sem.at[0])
+    own_rows = q_ref.at[pl.ds(l * ROWS, ROWS)]
+    own_q = pltpu.make_async_copy(own_rows, slots.at[0], local_sem.at[0])
     own_c = pltpu.make_async_copy(c_ref, cands.at[l], local_sem.at[1])
     own_id = pltpu.make_async_copy(id_ref, idents.at[l], local_sem.at[2])
 
@@ -120,46 +124,64 @@
     def hello(device):
         pl.semaphore_signal(barrier, inc=1, device_id=device, device_id_type=MESH)
 
-    @pl.when(early)
-    def _():
-        hello(at(ROW))
+    def when_z(*places):
+        hit = z == places[0]
+        for place in places[1:]:
+            hit = hit | (z == place)
+        return pl.when(hit)
+
+    @when_z(0, 3)
+    def _():
+        hello(at(ROW, over))
+
+    @when_z(2, 3)
+    def _():
+        hello(at(ROW - 1, over))
 
     @pl.when(z < ROW - 1)
     def _():
         hello(at(1))
 
-    for offset in (4, 5, 6, 7):
-
-        @pl.when(z + offset < ROW)
-        def _():
-            hello(at(offset))
+    for place, late in ((0, (4, 5, 6, 7)), (2, (5, 6, 7)), (3, (6, 7))):
+
+        @when_z(place)
+        def _():
+            for other in late:
+                hello(at(other - place))
 
     for k in (1, 2, 3):
         hello((i, l ^ k))
     own_q.start()
     own_id.start()
     own_c.start()
-    own_q.wait()
-    own_id.wait()
-    pl.semaphore_wait(barrier, jnp.where(early, 4 + jnp.where(z > 0, 1, 0), z + 1))
+    expected = jnp.where(z == 0, 4, jnp.where(z <= 4, 5, jnp.where(z == 5, 6, 7)))
+    pl.semaphore_wait(barrier, expected)
 
     def park_copy():
-        return remote(slots.at[0], slots.at[PARKED], park_send, slot_recv.at[PARKED], at(-ROW))
+        slot = jnp.where(z == 2, PARKED + 1, PARKED)
+        device = at(jnp.where(skew, 1 - ROW, -ROW), over)
+        return remote(own_rows, slots.at[slot], park_send, slot_recv.at[slot], device)
+
+    def first_copy():
+        return remote(own_rows, slots.at[1], chain_send.at[0], slot_recv.at[1], at(-1))
 
     def chain_copy(s):
         return remote(slots.at[s], slots.at[s + 1], chain_send.at[s], slot_recv.at[s + 1], at(-1))
 
-    def spread_copy(s):
-        return remote(slots.at[PARKED], slots.at[s], spread_send.at[s - 1], slot_recv.at[s], at(ROW - s))
+    def spread_copy(n, source, offset, slot):
+        return remote(slots.at[source], slots.at[slot], spread_send.at[n], slot_recv.at[slot], at(offset))
 
     def arrived(slot):
         remote(slots.at[0], slots.at[slot], park_send, slot_recv.at[slot], at(1)).wait_recv()
 
-    for e in range(4):
-
-        @pl.when(z >= 4 + e)
-        def _():
-            pl.semaphore_signal(ring_sem, inc=1, device_id=at(e - z), device_id_type=MESH)
+    for late, places in ((4, (0,)), (5, (0, 2)), (6, (0, 2, 3)), (7, (0, 2, 3))):
+
+        @when_z(late)
+        def _():
+            for place in places:
+                pl.semaphore_signal(
+                    ring_sem.at[late - 4], inc=1, device_id=at(place - late), device_id_type=MESH
+                )
 
     @pl.when(early)
     def _():
@@ -167,7 +189,7 @@
 
     @pl.when(z > 0)
     def _():
-        chain_copy(0).start()
+        first_copy().start()
 
     def across_copy(chunk, block):
         rows = pl.ds(chunk * CAND_PIECE, CAND_PIECE)
@@ -186,16 +208,27 @@
         )
 
     def id_copy(k, block):
-        return remote(
-            idents.at[block], idents.at[block], id_send.at[k - 1], id_recv.at[k - 1], (i, l ^ k)
-        )
-
+        return remote(id_ref, idents.at[block], id_send.at[k - 1], id_recv.at[k - 1], (i, l ^ k))
+
+    for k in (1, 2, 3):
+        id_copy(k, l).start()
     for chunk in range(CAND_CHUNKS):
         across_copy(chunk, l).start()
-    for k in (1, 2, 3):
-        id_copy(k, l).start()
     beside_copy(l).start()
 
+    @pl.when((z > 0) & (z < ROW - 1))
+    def _():
+        arrived(1)
+        chain_copy(1).start()
+
+    @when_z(0)
+    def _():
+        arrived(PARKED)
+        for n, late in enumerate((7, 6, 4, 5)):
+            pl.semaphore_wait(ring_sem.at[late - 4], 1)
+            spread_copy(n, PARKED, late, 8 - late).start()
+
+    own_id.wait()
     for k in (1, 2, 3):
         id_copy(k, l ^ k).wait_recv()
     lane = lax.broadcasted_iota(jnp.int32, (CB, 128), 1)
@@ -222,24 +255,52 @@
             total += jnp.sum(jnp.where(column == lane + 128 * a, ident, 0.0), 0, keepdims=True)
         table[a] = jnp.broadcast_to(total, (8, 128)).astype(jnp.int32)
 
-    @pl.when((z > 0) & (z < ROW - 1))
-    def _():
-        arrived(1)
-        chain_copy(1).start()
-
-    @pl.when(early)
-    def _():
-        arrived(PARKED)
-        pl.semaphore_wait(ring_sem, 4 - z)
-        for s in (4, 3, 2, 1):
-
-            @pl.when(s > z)
-            def _():
-                spread_copy(s).start()
-
     for chunk in range(CAND_CHUNKS):
         across_copy(chunk, l ^ 2).wait_recv()
         onward_copy(chunk, l ^ 2).start()
+
+    @when_z(0)
+    def _():
+        arrived(2)
+        for n in range(3):
+            spread_copy(n, PARKED, 4, 4).wait_send()
+        pl.semaphore_signal(go_sem, inc=1, device_id=at(2), device_id_type=MESH)
+
+    @when_z(2)
+    def _():
+        for late in (5, 6, 7):
+            pl.semaphore_wait(ring_sem.at[late - 4], 1)
+        arrived(PARKED)
+        spread_copy(0, PARKED, 3, 4).start()
+
+    @when_z(3)
+    def _():
+        for late in (6, 7):
+            pl.semaphore_wait(ring_sem.at[late - 4], 1)
+        arrived(PARKED + 1)
+        spread_copy(0, PARKED + 1, 3, 4).start()
+
+    @pl.when((z > 0) & (z < ROW - 2))
+    def _():
+        arrived(2)
+        chain_copy(2).start()
+
+    @when_z(2)
+    def _():
+        pl.semaphore_wait(go_sem, 1)
+        spread_copy(1, PARKED, 4, 3).start()
+        spread_copy(2, PARKED, 5, 2).start()
+        spread_copy(1, PARKED, 4, 3).wait_send()
+        pl.semaphore_signal(go_sem, inc=1, device_id=at(1), device_id_type=MESH)
+
+    @when_z(3)
+    def _():
+        pl.semaphore_wait(go_sem, 1)
+        spread_copy(1, PARKED + 1, 4, 3).start()
+        arrived(PARKED)
+        spread_copy(2, PARKED, 4, 4).start()
+
+    own_q.wait()
     own_c.wait()
     beside_copy(l ^ 1).wait_recv()
     for chunk in range(CAND_CHUNKS):
@@ -254,23 +315,27 @@
 
     def result_copy(s):
         return remote(
-            outbox.at[s], inbox.at[s - 1], res_send.at[s - 1], res_recv.at[s - 1], at(s)
+            outbox.at[s], inbox.at[s - 1], res_send.at[s - 1], res_recv.at[s - 1],
+            at(s, jnp.where(z + s >= ROW, over, l)),
         )
 
     def step(t, carry):
-        s = jnp.where(
-            (z == 4) & (t >= 2),
-            jnp.where(t == 2, 4, t - 1),
-            jnp.where((z == 5) & ((t == 2) | (t == 3)), 5 - t, t),
-        )
-
-        @pl.when((s >= 2) | ((s == 1) & ((z == 0) | (z == ROW - 1))))
+        s = jnp.where(z == 4, lax.rem(t + 4, 5), jnp.where(z == 5, lax.rem(t + 3, 5), t))
+        s = jnp.where(z == 6, jnp.where(t == 0, 2, jnp.where(t < 3, t - 1, 7 - t)), s)
+        s = jnp.where((z == 7) & (t < 2), 1 - t, s)
+
+        chained = (z > 0) & (z < 5)
+
+        @pl.when(chained & (t == jnp.where(z == 4, 2, 1)))
+        def _():
+            arrived(3)
+            chain_copy(3).start()
+
+        late_slot = ((s == 3) & ~chained) | (s == 4)
+
+        @pl.when(late_slot | ((s == 2) & (z >= 6)) | ((s == 1) & ((z == 0) | (z == ROW - 1))))
         def _():
             arrived(s)
-
-        @pl.when((z > 0) & (s >= 2) & (s <= 3) & (s + z < ROW))
-        def _():
-            chain_copy(s).start()
 
         block = slots[s]
         four = jnp.concatenate([block] * 4, 0)
@@ -291,7 +356,8 @@
                 keys[31 - k : 32 - k, :] = v[k][0:1, :]
                 keys[15 - k : 16 - k, :] = v[k][4:5, :]
 
-        left = lax.broadcasted_iota(jnp.int32, (8, 128), 1) < ROWS
+        lanes = lax.broadcasted_iota(jnp.int32, (8, 128), 1)
+        both = []
         for g in range(4):
             key = keys[8 * g : 8 * g + 8, :]
             place = key & 127
@@ -300,7 +366,9 @@
             ident = jnp.where(
                 which < 2, jnp.where(which == 0, found[0], found[1]), jnp.where(which == 2, found[2], found[3])
             )
-            outbox[s, 8 * g : 8 * g + 8, :] = jnp.where(left, key >> 9, pltpu.roll(ident, ROWS, 1))
+            both.append(jnp.where(lanes < ROWS, key >> 9, pltpu.roll(ident, ROWS, 1)))
+        for g in range(2):
+            outbox[s, 8 * g : 8 * g + 8, :] = jnp.where(lanes < 64, both[g], pltpu.roll(both[g + 2], 64, 1))
 
         @pl.when(s > 0)
         def _():
@@ -311,7 +379,8 @@
     lax.fori_loop(0, STEPS + 1, step, 0)
 
     def pair(x):
-        return [x, pltpu.roll(x, 128 - ROWS, 1)]
+        whole = jnp.concatenate([x, pltpu.roll(x, 64, 1)], 0)
+        return [whole, pltpu.roll(whole, 128 - ROWS, 1)]
 
     best = pair(outbox[0])
     for s in range(1, STEPS + 1):
@@ -331,9 +400,11 @@
         def _():
             chain_copy(s - 1).wait_send()
 
-        @pl.when(early & (s > z))
-        def _():
-            spread_copy(s).wait_send()
+    for n, places in enumerate(((2, 3), (3,), (2, 3), (0,))):
+
+        @when_z(*places)
+        def _():
+            spread_copy(n, PARKED, 4, 4).wait_send()
 
     for k in (1, 2, 3):
         id_copy(k, l).wait_send()
@@ -360,17 +431,17 @@
         in_specs=[any_space, any_space, any_space],
         out_specs=(vmem, vmem),
         scratch_shapes=[
-            pltpu.VMEM((PARKED + 1, ROWS, D), jnp.bfloat16),
+            pltpu.VMEM((PARKED + 2, ROWS, D), jnp.bfloat16),
             pltpu.VMEM((LAYERS, CB, D), jnp.bfloat16),
             pltpu.VMEM((LAYERS, 1, CB), jnp.int32),
             pltpu.VMEM((CB, 128), jnp.int32),
             pltpu.VMEM((4, 8, 128), jnp.int32),
             pltpu.VMEM((K, 128), jnp.int32),
-            pltpu.VMEM((STEPS + 1, K, 128), jnp.int32),
-            pltpu.VMEM((STEPS, K, 128), jnp.int32),
+            pltpu.VMEM((STEPS + 1, K // 2, 128), jnp.int32),
+            pltpu.VMEM((STEPS, K // 2, 128), jnp.int32),
             dma((3,)),
             dma((STEPS,)),
-            dma((PARKED + 1,)),
+            dma((PARKED + 2,)),
             dma,
             dma((STEPS,)),
             dma((3, CAND_CHUNKS)),
@@ -379,6 +450,7 @@
             dma((3,)),
             dma((STEPS,)),
             dma((STEPS,)),
+            pltpu.SemaphoreType.REGULAR((4,)),
             pltpu.SemaphoreType.REGULAR,
         ],
         compiler_params=pltpu.CompilerParams(

time: 33.1 us -> 31.6 us (0.955)
  Pallas kernels: 31.1 us -> 29.3 us
    pallas_call x1, Pallas kernels: 31.1 us -> 29.3 us  [shards(): pl.pallas_call(kernel, out_shape=(jax.ShapeDtypeStruct((ROWS, K), jnp.flo...]
where the time goes in v3:
time: 31.6 us; the launch traced here: 31.1 us
  Pallas kernels  29.3 us (93%)
  local copies, waits for them, and re-layouts  1.21 us (4%)
  between operations  0.64 us (2%)
    pallas_call x1, Pallas kernels, shards(): pl.pallas_call(kernel, out_shape=(jax.ShapeDtypeStruct((ROWS, K), jnp.flo...  29.3 us
    unnamed x2, local copies, waits for them, and re-layouts  1.21 us

profile of v3, /device:TPU:64, one launch (start us, length us, event | category | flops | bytes accessed | tf_op | source)
XLA Modules:
  0.0 31.1 jit_solution(10270858067430397759)
XLA Ops:
  0.6 29.3 %shard_map.50 = (f32[32,32]{1,0:T(8,128)S(1)}, s32[32,32]{1,0:T(8,128)S(1)}) custom-call(bf16[128,768]{1,0:T(8,128)(2,1)} %q_ref.1, bf16[128,768]{1,0:T(8,128)(2,1)} %c_ref.1, s32[1,128]{1,0:T(1,128)} %bitcast.1), custom_call_target="tpu_custom_call" | custom-call | tf_op jit(solution)/shard_map/pallas_call | solution.py:425
  29.9 0.6 %copy.7 = f32[32,32]{1,0:T(8,128)} copy(f32[32,32]{1,0:T(8,128)S(1)} %get-tuple-element.4) | data formatting | bytes 8192
  30.5 0.6 %copy.8 = s32[32,32]{1,0:T(8,128)} copy(s32[32,32]{1,0:T(8,128)S(1)} %get-tuple-element.5) | data formatting | bytes 8192

commit v4 on v3

--- a/solution.py
+++ b/solution.py
@@ -94,10 +94,10 @@
 
 
 def kernel(
-    q_ref, c_ref, id_ref, dist_ref, near_ref,
+    q_ref, c_ref, id_ref, out_ref,
     slots, cands, idents, base, table, keys, outbox, inbox,
     local_sem, chain_send, slot_recv, park_send, spread_send, cand_send, cand_recv, id_send, id_recv,
-    res_send, res_recv, ring_sem, go_sem,
+    res_send, res_recv, ring_sem,
 ):
     i, l = lax.axis_index("loop"), lax.axis_index("layer")
     z = lax.rem(i, ROW)
@@ -108,6 +108,8 @@
         return (lax.rem(i + offset + 2 * LOOP, LOOP), layer)
 
     over = l ^ 2
+    keeper = (l & 1) == 1
+    lower = l & 2
 
     def remote(src, dst, send, recv, device):
         return pltpu.make_async_remote_copy(
@@ -130,13 +132,21 @@
             hit = hit | (z == place)
         return pl.when(hit)
 
-    @when_z(0, 3)
+    def when_keeper(*places):
+        hit = z == places[0]
+        for place in places[1:]:
+            hit = hit | (z == place)
+        return pl.when(hit & keeper)
+
+    @when_keeper(0, 3)
     def _():
         hello(at(ROW, over))
-
-    @when_z(2, 3)
+        hello(at(ROW, over ^ 1))
+
+    @when_keeper(2, 3)
     def _():
         hello(at(ROW - 1, over))
+        hello(at(ROW - 1, over ^ 1))
 
     @pl.when(z < ROW - 1)
     def _():
@@ -144,10 +154,11 @@
 
     for place, late in ((0, (4, 5, 6, 7)), (2, (5, 6, 7)), (3, (6, 7))):
 
-        @when_z(place)
+        @when_keeper(place)
         def _():
             for other in late:
                 hello(at(other - place))
+                hello(at(other - place, lower))
 
     for k in (1, 2, 3):
         hello((i, l ^ k))
@@ -158,9 +169,9 @@
     pl.semaphore_wait(barrier, expected)
 
     def park_copy():
-        slot = jnp.where(z == 2, PARKED + 1, PARKED)
-        device = at(jnp.where(skew, 1 - ROW, -ROW), over)
-        return remote(own_rows, slots.at[slot], park_send, slot_recv.at[slot], device)
+        slot = jnp.where(z == 2, PARKED + 1, PARKED) + jnp.where(keeper, 0, 2)
+        device = at(jnp.where(skew, 1 - ROW, -ROW), over | 1)
+        return remote(slots.at[0], slots.at[slot], park_send, slot_recv.at[slot], device)
 
     def first_copy():
         return remote(own_rows, slots.at[1], chain_send.at[0], slot_recv.at[1], at(-1))
@@ -171,6 +182,11 @@
     def spread_copy(n, source, offset, slot):
         return remote(slots.at[source], slots.at[slot], spread_send.at[n], slot_recv.at[slot], at(offset))
 
+    def lower_copy(n, source, offset, slot):
+        return remote(
+            slots.at[source + 2], slots.at[slot], spread_send.at[n + 4], slot_recv.at[slot], at(offset, lower)
+        )
+
     def arrived(slot):
         remote(slots.at[0], slots.at[slot], park_send, slot_recv.at[slot], at(1)).wait_recv()
 
@@ -180,8 +196,10 @@
         def _():
             for place in places:
                 pl.semaphore_signal(
-                    ring_sem.at[late - 4], inc=1, device_id=at(place - late), device_id_type=MESH
+                    ring_sem.at[late - 4], inc=1, device_id=at(place - late, l | 1), device_id_type=MESH
                 )
+
+    own_q.wait()
 
     @pl.when(early)
     def _():
@@ -221,12 +239,15 @@
         arrived(1)
         chain_copy(1).start()
 
-    @when_z(0)
+    @when_keeper(0)
     def _():
         arrived(PARKED)
         for n, late in enumerate((7, 6, 4, 5)):
-            pl.semaphore_wait(ring_sem.at[late - 4], 1)
+            pl.semaphore_wait(ring_sem.at[late - 4], 2)
             spread_copy(n, PARKED, late, 8 - late).start()
+        arrived(PARKED + 2)
+        for n, late in enumerate((7, 6, 4, 5)):
+            lower_copy(n, PARKED, late, 8 - late).start()
 
     own_id.wait()
     for k in (1, 2, 3):
@@ -259,48 +280,33 @@
         across_copy(chunk, l ^ 2).wait_recv()
         onward_copy(chunk, l ^ 2).start()
 
-    @when_z(0)
-    def _():
-        arrived(2)
-        for n in range(3):
-            spread_copy(n, PARKED, 4, 4).wait_send()
-        pl.semaphore_signal(go_sem, inc=1, device_id=at(2), device_id_type=MESH)
-
-    @when_z(2)
+    @when_keeper(2)
     def _():
         for late in (5, 6, 7):
-            pl.semaphore_wait(ring_sem.at[late - 4], 1)
+            pl.semaphore_wait(ring_sem.at[late - 4], 2)
         arrived(PARKED)
-        spread_copy(0, PARKED, 3, 4).start()
-
-    @when_z(3)
+        for n, (offset, slot) in enumerate(((3, 4), (4, 3), (5, 2))):
+            spread_copy(n, PARKED, offset, slot).start()
+        arrived(PARKED + 2)
+        for n, (offset, slot) in enumerate(((3, 4), (4, 3), (5, 2))):
+            lower_copy(n, PARKED, offset, slot).start()
+
+    @when_keeper(3)
     def _():
         for late in (6, 7):
-            pl.semaphore_wait(ring_sem.at[late - 4], 1)
-        arrived(PARKED + 1)
-        spread_copy(0, PARKED + 1, 3, 4).start()
+            pl.semaphore_wait(ring_sem.at[late - 4], 2)
+        for copy, extra in ((spread_copy, 0), (lower_copy, 2)):
+            arrived(PARKED + extra)
+            copy(0, PARKED, 4, 4).start()
+            arrived(PARKED + 1 + extra)
+            copy(1, PARKED + 1, 3, 4).start()
+            copy(2, PARKED + 1, 4, 3).start()
 
     @pl.when((z > 0) & (z < ROW - 2))
     def _():
         arrived(2)
         chain_copy(2).start()
 
-    @when_z(2)
-    def _():
-        pl.semaphore_wait(go_sem, 1)
-        spread_copy(1, PARKED, 4, 3).start()
-        spread_copy(2, PARKED, 5, 2).start()
-        spread_copy(1, PARKED, 4, 3).wait_send()
-        pl.semaphore_signal(go_sem, inc=1, device_id=at(1), device_id_type=MESH)
-
-    @when_z(3)
-    def _():
-        pl.semaphore_wait(go_sem, 1)
-        spread_copy(1, PARKED + 1, 4, 3).start()
-        arrived(PARKED)
-        spread_copy(2, PARKED, 4, 4).start()
-
-    own_q.wait()
     own_c.wait()
     beside_copy(l ^ 1).wait_recv()
     for chunk in range(CAND_CHUNKS):
@@ -333,7 +339,7 @@
 
         late_slot = ((s == 3) & ~chained) | (s == 4)
 
-        @pl.when(late_slot | ((s == 2) & (z >= 6)) | ((s == 1) & ((z == 0) | (z == ROW - 1))))
+        @pl.when(late_slot | ((s == 2) & ((z == 0) | (z >= 6))) | ((s == 1) & ((z == 0) | (z == ROW - 1))))
         def _():
             arrived(s)
 
@@ -378,33 +384,17 @@
 
     lax.fori_loop(0, STEPS + 1, step, 0)
 
-    def pair(x):
-        whole = jnp.concatenate([x, pltpu.roll(x, 64, 1)], 0)
-        return [whole, pltpu.roll(whole, 128 - ROWS, 1)]
-
-    best = pair(outbox[0])
     for s in range(1, STEPS + 1):
-        result_copy(s).wait_recv()
-        best = merged(best, pair(inbox[s - 1]))
-    block = slots[0]
-    own = lax.dot_general(ones, jnp.concatenate([block * block] * 4, 0), NT, preferred_element_type=jnp.float32)
-    dist = (best[0].astype(jnp.float32) + own[:K, :]) * (0.125 / D)
-    both = jnp.concatenate([dist, best[1].astype(jnp.float32), dist, dist], 0).T
-    dist_ref[...] = both[:ROWS, :K]
-    near_ref[...] = both[:ROWS, K : 2 * K].astype(jnp.int32)
-
-    for s in range(1, STEPS + 1):
-        result_copy(s).wait_send()
-
         @pl.when((z > 0) & (s - 1 + z < ROW))
         def _():
             chain_copy(s - 1).wait_send()
 
-    for n, places in enumerate(((2, 3), (3,), (2, 3), (0,))):
-
-        @when_z(*places)
+    for n, places in enumerate(((0, 2, 3), (0, 2, 3), (0, 2, 3), (0,))):
+
+        @when_keeper(*places)
         def _():
             spread_copy(n, PARKED, 4, 4).wait_send()
+            lower_copy(n, PARKED, 4, 4).wait_send()
 
     for k in (1, 2, 3):
         id_copy(k, l).wait_send()
@@ -417,21 +407,34 @@
     def _():
         park_copy().wait_send()
 
+    def pair(x):
+        whole = jnp.concatenate([x, pltpu.roll(x, 64, 1)], 0)
+        return [whole, pltpu.roll(whole, 128 - ROWS, 1)]
+
+    block = slots[0]
+    own = lax.dot_general(ones, jnp.concatenate([block * block] * 4, 0), NT, preferred_element_type=jnp.float32)
+    best = pair(outbox[0])
+    for s in range(1, STEPS + 1):
+        result_copy(s).wait_recv()
+        best = merged(best, pair(inbox[s - 1]))
+    dist = (best[0].astype(jnp.float32) + own[:K, :]) * (0.125 / D)
+    both = jnp.concatenate([dist, best[1].astype(jnp.float32), dist, dist], 0).T
+    out_ref[...] = both[:ROWS, :]
+    for s in range(1, STEPS + 1):
+        result_copy(s).wait_send()
+
 
 def shards(queries, candidates, cand_ids):
     dma = pltpu.SemaphoreType.DMA
     any_space = pl.BlockSpec(memory_space=pltpu.HBM)
     vmem = pl.BlockSpec(memory_space=pltpu.VMEM)
-    return pl.pallas_call(
+    lists = pl.pallas_call(
         kernel,
-        out_shape=(
-            jax.ShapeDtypeStruct((ROWS, K), jnp.float32),
-            jax.ShapeDtypeStruct((ROWS, K), jnp.int32),
-        ),
+        out_shape=jax.ShapeDtypeStruct((ROWS, 128), jnp.float32),
         in_specs=[any_space, any_space, any_space],
-        out_specs=(vmem, vmem),
+        out_specs=vmem,
         scratch_shapes=[
-            pltpu.VMEM((PARKED + 2, ROWS, D), jnp.bfloat16),
+            pltpu.VMEM((PARKED + 4, ROWS, D), jnp.bfloat16),
             pltpu.VMEM((LAYERS, CB, D), jnp.bfloat16),
             pltpu.VMEM((LAYERS, 1, CB), jnp.int32),
             pltpu.VMEM((CB, 128), jnp.int32),
@@ -441,9 +444,9 @@
             pltpu.VMEM((STEPS, K // 2, 128), jnp.int32),
             dma((3,)),
             dma((STEPS,)),
-            dma((PARKED + 2,)),
+            dma((PARKED + 4,)),
             dma,
-            dma((STEPS,)),
+            dma((8,)),
             dma((3, CAND_CHUNKS)),
             dma((3, CAND_CHUNKS)),
             dma((3,)),
@@ -451,12 +454,12 @@
             dma((STEPS,)),
             dma((STEPS,)),
             pltpu.SemaphoreType.REGULAR((4,)),
-            pltpu.SemaphoreType.REGULAR,
         ],
         compiler_params=pltpu.CompilerParams(
             collective_id=0, has_side_effects=True, vmem_limit_bytes=16 * 1024 * 1024
         ),
     )(*(pltpu.with_memory_space_constraint(x, pltpu.HBM) for x in (queries, candidates, cand_ids.reshape(1, CB))))
+    return lists[:, :K], lists[:, K : 2 * K].astype(jnp.int32)
 
 
 def solution(mesh):

time: 31.6 us -> 29.7 us (0.940)
  the two profiles are of different devices: /device:TPU:64 before, /device:TPU:32 now
where the time goes in v4:
time: 29.7 us; the launch traced here: 29.6 us
  Pallas kernels  28.3 us (95%)
  other arithmetic  0.68 us (2%)
  between operations  0.64 us (2%)
    pallas_call x1, Pallas kernels, shards(): pl.pallas_call(kernel, out_shape=jax.ShapeDtypeStruct((ROWS, 128), jnp.fl...  28.3 us
    convert_element_type x1, other arithmetic, shards(): return (lists[:, :K], lists[:, K:2 * K].astype(jnp.int32))  0.68 us

profile of v4, /device:TPU:32, one launch (start us, length us, event | category | flops | bytes accessed | tf_op | source)
XLA Modules:
  0.0 29.6 jit_solution(11992949894525482747)
XLA Ops:
  0.6 28.3 %shard_map.50 = f32[32,128]{1,0:T(8,128)S(1)} custom-call(bf16[128,768]{1,0:T(8,128)(2,1)} %q_ref.1, bf16[128,768]{1,0:T(8,128)(2,1)} %c_ref.1, s32[1,128]{1,0:T(1,128)} %bitcast.1), custom_call_target="tpu_custom_call" | custom-call | tf_op jit(solution)/shard_map/pallas_call | solution.py:431
  28.9 0.7 %slice_convert_fusion = (s32[32,32]{1,0:T(8,128)}, f32[32,32]{1,0:T(8,128)}) fusion(f32[32,128]{1,0:T(8,128)S(1)} %shard_map.50), kind=kLoop, calls=%fused_computation | loop fusion | flops 1024 | bytes 16384 | tf_op jit(solution)/shard_map/convert_element_type | solution.py:462

commit v5 on v4

--- a/solution.py
+++ b/solution.py
@@ -14,7 +14,7 @@
 CB = 128
 ROWS = 32
 PARKED = 5
-CAND_CHUNKS = 8
+CAND_CHUNKS = 4
 CAND_PIECE = CB // CAND_CHUNKS
 MESH = pl.DeviceIdType.MESH
 NT = (((1,), (1,)), ((), ()))
@@ -138,15 +138,15 @@
             hit = hit | (z == place)
         return pl.when(hit & keeper)
 
+    @when_keeper(2, 3)
+    def _():
+        hello(at(ROW - 1, over))
+        hello(at(ROW - 1, over ^ 1))
+
     @when_keeper(0, 3)
     def _():
         hello(at(ROW, over))
         hello(at(ROW, over ^ 1))
-
-    @when_keeper(2, 3)
-    def _():
-        hello(at(ROW - 1, over))
-        hello(at(ROW - 1, over ^ 1))
 
     @pl.when(z < ROW - 1)
     def _():
@@ -159,13 +159,17 @@
             for other in late:
                 hello(at(other - place))
                 hello(at(other - place, lower))
+
+    @when_z(0)
+    def _():
+        hello(at(4))
 
     for k in (1, 2, 3):
         hello((i, l ^ k))
     own_q.start()
     own_id.start()
     own_c.start()
-    expected = jnp.where(z == 0, 4, jnp.where(z <= 4, 5, jnp.where(z == 5, 6, 7)))
+    expected = jnp.where(z == 0, 4, jnp.where(early, 5, jnp.where(z == 4, 6, jnp.where(z == 5, 6, 7))))
     pl.semaphore_wait(barrier, expected)
 
     def park_copy():
@@ -187,6 +191,9 @@
             slots.at[source + 2], slots.at[slot], spread_send.at[n + 4], slot_recv.at[slot], at(offset, lower)
         )
 
+    def jump_copy():
+        return remote(slots.at[0], slots.at[4], chain_send.at[4], slot_recv.at[4], at(-4))
+
     def arrived(slot):
         remote(slots.at[0], slots.at[slot], park_send, slot_recv.at[slot], at(1)).wait_recv()
 
@@ -208,6 +215,10 @@
     @pl.when(z > 0)
     def _():
         first_copy().start()
+
+    @when_z(4)
+    def _():
+        jump_copy().start()
 
     def across_copy(chunk, block):
         rows = pl.ds(chunk * CAND_PIECE, CAND_PIECE)
@@ -242,12 +253,11 @@
     @when_keeper(0)
     def _():
         arrived(PARKED)
-        for n, late in enumerate((7, 6, 4, 5)):
+        arrived(PARKED + 2)
+        for n, late in enumerate((7, 6, 5, 4)):
             pl.semaphore_wait(ring_sem.at[late - 4], 2)
+            lower_copy(n, PARKED, late, 8 - late).start()
             spread_copy(n, PARKED, late, 8 - late).start()
-        arrived(PARKED + 2)
-        for n, late in enumerate((7, 6, 4, 5)):
-            lower_copy(n, PARKED, late, 8 - late).start()
 
     own_id.wait()
     for k in (1, 2, 3):
@@ -285,39 +295,46 @@
         for late in (5, 6, 7):
             pl.semaphore_wait(ring_sem.at[late - 4], 2)
         arrived(PARKED)
-        for n, (offset, slot) in enumerate(((3, 4), (4, 3), (5, 2))):
+        arrived(PARKED + 2)
+        for n, (offset, slot) in enumerate(((5, 2), (4, 3), (3, 4))):
+            lower_copy(n, PARKED, offset, slot).start()
             spread_copy(n, PARKED, offset, slot).start()
-        arrived(PARKED + 2)
-        for n, (offset, slot) in enumerate(((3, 4), (4, 3), (5, 2))):
-            lower_copy(n, PARKED, offset, slot).start()
 
     @when_keeper(3)
     def _():
         for late in (6, 7):
             pl.semaphore_wait(ring_sem.at[late - 4], 2)
-        for copy, extra in ((spread_copy, 0), (lower_copy, 2)):
-            arrived(PARKED + extra)
-            copy(0, PARKED, 4, 4).start()
-            arrived(PARKED + 1 + extra)
-            copy(1, PARKED + 1, 3, 4).start()
-            copy(2, PARKED + 1, 4, 3).start()
+        arrived(PARKED + 1)
+        arrived(PARKED + 3)
+        lower_copy(1, PARKED + 1, 4, 3).start()
+        lower_copy(0, PARKED + 1, 3, 4).start()
+        spread_copy(1, PARKED + 1, 4, 3).start()
+        spread_copy(0, PARKED + 1, 3, 4).start()
+        arrived(PARKED)
+        spread_copy(2, PARKED, 4, 4).start()
+        arrived(PARKED + 2)
+        lower_copy(2, PARKED, 4, 4).start()
 
     @pl.when((z > 0) & (z < ROW - 2))
     def _():
         arrived(2)
         chain_copy(2).start()
 
+    ones = jnp.ones((128, D), jnp.bfloat16)
+    group = lax.broadcasted_iota(jnp.int32, (CB, 128), 1) // ROWS
+
+    def norms(m, total):
+        block = cands[m]
+        found = lax.dot_general(block * block, ones, NT, preferred_element_type=jnp.float32)
+        return jnp.where(group == m, found, total)
+
     own_c.wait()
+    total = norms(l, jnp.zeros((CB, 128), jnp.float32))
     beside_copy(l ^ 1).wait_recv()
+    total = norms(l ^ 2, norms(l ^ 1, total))
     for chunk in range(CAND_CHUNKS):
         onward_copy(chunk, l ^ 3).wait_recv()
-
-    ones = jnp.ones((128, D), jnp.bfloat16)
-    norms = []
-    for m in range(LAYERS):
-        block = cands[m]
-        norms.append(lax.dot_general(block * block, ones, NT, preferred_element_type=jnp.float32))
-    base[...] = by_layer(norms).astype(jnp.int32) * 512 + rank
+    base[...] = norms(l ^ 3, total).astype(jnp.int32) * 512 + rank
 
     def result_copy(s):
         return remote(
@@ -327,10 +344,10 @@
 
     def step(t, carry):
         s = jnp.where(z == 4, lax.rem(t + 4, 5), jnp.where(z == 5, lax.rem(t + 3, 5), t))
-        s = jnp.where(z == 6, jnp.where(t == 0, 2, jnp.where(t < 3, t - 1, 7 - t)), s)
+        s = jnp.where((z == 6) & (t < 3), jnp.where(t == 0, 2, t - 1), s)
         s = jnp.where((z == 7) & (t < 2), 1 - t, s)
 
-        chained = (z > 0) & (z < 5)
+        chained = (z > 1) & (z < 5)
 
         @pl.when(chained & (t == jnp.where(z == 4, 2, 1)))
         def _():
@@ -362,19 +379,17 @@
                 keys[31 - k : 32 - k, :] = v[k][0:1, :]
                 keys[15 - k : 16 - k, :] = v[k][4:5, :]
 
-        lanes = lax.broadcasted_iota(jnp.int32, (8, 128), 1)
-        both = []
-        for g in range(4):
-            key = keys[8 * g : 8 * g + 8, :]
-            place = key & 127
-            which = (key >> 7) & 3
-            found = [jnp.take_along_axis(table[a], place, axis=1, mode="promise_in_bounds") for a in range(4)]
-            ident = jnp.where(
-                which < 2, jnp.where(which == 0, found[0], found[1]), jnp.where(which == 2, found[2], found[3])
-            )
-            both.append(jnp.where(lanes < ROWS, key >> 9, pltpu.roll(ident, ROWS, 1)))
-        for g in range(2):
-            outbox[s, 8 * g : 8 * g + 8, :] = jnp.where(lanes < 64, both[g], pltpu.roll(both[g + 2], 64, 1))
+        group = lax.broadcasted_iota(jnp.int32, (8, 128), 1) // ROWS
+        key = keys[0:8, :]
+        for g in (1, 2, 3):
+            key = jnp.where(group == g, pltpu.roll(keys[8 * g : 8 * g + 8, :], ROWS * g, 1), key)
+        place = key & 127
+        which = (key >> 7) & 3
+        found = [jnp.take_along_axis(table[a], place, axis=1, mode="promise_in_bounds") for a in range(4)]
+        outbox[s, 0:8, :] = key >> 9
+        outbox[s, 8:16, :] = jnp.where(
+            which < 2, jnp.where(which == 0, found[0], found[1]), jnp.where(which == 2, found[2], found[3])
+        )
 
         @pl.when(s > 0)
         def _():
@@ -385,7 +400,7 @@
     lax.fori_loop(0, STEPS + 1, step, 0)
 
     for s in range(1, STEPS + 1):
-        @pl.when((z > 0) & (s - 1 + z < ROW))
+        @pl.when((z > 0) & (s - 1 + z < ROW) & ((z > 1) | (s < 4)))
         def _():
             chain_copy(s - 1).wait_send()
 
@@ -407,9 +422,16 @@
     def _():
         park_copy().wait_send()
 
+    @when_z(4)
+    def _():
+        jump_copy().wait_send()
+
+    for s in range(1, STEPS + 1):
+        result_copy(s).wait_send()
+
     def pair(x):
-        whole = jnp.concatenate([x, pltpu.roll(x, 64, 1)], 0)
-        return [whole, pltpu.roll(whole, 128 - ROWS, 1)]
+        turns = [x] + [pltpu.roll(x, 128 - ROWS * g, 1) for g in (1, 2, 3)]
+        return [jnp.concatenate([turn[h : h + 8] for turn in turns], 0) for h in (0, 8)]
 
     block = slots[0]
     own = lax.dot_general(ones, jnp.concatenate([block * block] * 4, 0), NT, preferred_element_type=jnp.float32)
@@ -420,8 +442,6 @@
     dist = (best[0].astype(jnp.float32) + own[:K, :]) * (0.125 / D)
     both = jnp.concatenate([dist, best[1].astype(jnp.float32), dist, dist], 0).T
     out_ref[...] = both[:ROWS, :]
-    for s in range(1, STEPS + 1):
-        result_copy(s).wait_send()
 
 
 def shards(queries, candidates, cand_ids):
@@ -443,7 +463,7 @@
             pltpu.VMEM((STEPS + 1, K // 2, 128), jnp.int32),
             pltpu.VMEM((STEPS, K // 2, 128), jnp.int32),
             dma((3,)),
-            dma((STEPS,)),
+            dma((STEPS + 1,)),
             dma((PARKED + 4,)),
             dma,
             dma((8,)),

time: 29.7 us -> 27.3 us (0.919)
  the two profiles are of different devices: /device:TPU:32 before, /device:TPU:64 now
where the time goes in v5:
time: 27.3 us; the launch traced here: 27.2 us
  Pallas kernels  25.9 us (95%)
  other arithmetic  0.68 us (2%)
  between operations  0.64 us (2%)
    pallas_call x1, Pallas kernels, shards(): pl.pallas_call(kernel, out_shape=jax.ShapeDtypeStruct((ROWS, 128), jnp.fl...  25.9 us
    convert_element_type x1, other arithmetic, shards(): return (lists[:, :K], lists[:, K:2 * K].astype(jnp.int32))  0.68 us

profile of v5, /device:TPU:64, one launch (start us, length us, event | category | flops | bytes accessed | tf_op | source)
XLA Modules:
  0.0 27.2 jit_solution(2664898333576437548)
XLA Ops:
  0.6 25.9 %shard_map.50 = f32[32,128]{1,0:T(8,128)S(1)} custom-call(bf16[128,768]{1,0:T(8,128)(2,1)} %q_ref.1, bf16[128,768]{1,0:T(8,128)(2,1)} %c_ref.1, s32[1,128]{1,0:T(1,128)} %bitcast.1), custom_call_target="tpu_custom_call" | custom-call | tf_op jit(solution)/shard_map/pallas_call | solution.py:451
  26.5 0.7 %slice_convert_fusion = (s32[32,32]{1,0:T(8,128)}, f32[32,32]{1,0:T(8,128)}) fusion(f32[32,128]{1,0:T(8,128)S(1)} %shard_map.50), kind=kLoop, calls=%fused_computation | loop fusion | flops 1024 | bytes 16384 | tf_op jit(solution)/shard_map/convert_element_type | solution.py:482

commit v6 on v5

--- a/solution.py
+++ b/solution.py
@@ -14,8 +14,8 @@
 CB = 128
 ROWS = 32
 PARKED = 5
-CAND_CHUNKS = 4
-CAND_PIECE = CB // CAND_CHUNKS
+CAND_PIECES = ((0, 48), (48, 32), (80, 32), (112, 16))
+CAND_CHUNKS = len(CAND_PIECES)
 MESH = pl.DeviceIdType.MESH
 NT = (((1,), (1,)), ((), ()))
 
@@ -221,7 +221,7 @@
         jump_copy().start()
 
     def across_copy(chunk, block):
-        rows = pl.ds(chunk * CAND_PIECE, CAND_PIECE)
+        rows = pl.ds(*CAND_PIECES[chunk])
         return remote(
             c_ref.at[rows], cands.at[block, rows], cand_send.at[0, chunk], cand_recv.at[0, chunk], (i, l ^ 2)
         )
@@ -230,7 +230,7 @@
         return remote(c_ref, cands.at[block], cand_send.at[1, 0], cand_recv.at[1, 0], (i, l ^ 1))
 
     def onward_copy(chunk, block):
-        rows = pl.ds(chunk * CAND_PIECE, CAND_PIECE)
+        rows = pl.ds(*CAND_PIECES[chunk])
         return remote(
             cands.at[block, rows], cands.at[block, rows],
             cand_send.at[2, chunk], cand_recv.at[2, chunk], (i, l ^ 1),

time: 27.3 us -> 27.3 us (level)
  no operation moved by 1% of the time
where the time goes in v6:
time: 27.3 us; the launch traced here: 27.2 us
  Pallas kernels  25.9 us (95%)
  other arithmetic  0.68 us (2%)
  between operations  0.64 us (2%)
    pallas_call x1, Pallas kernels, shards(): pl.pallas_call(kernel, out_shape=jax.ShapeDtypeStruct((ROWS, 128), jnp.fl...  25.9 us
    convert_element_type x1, other arithmetic, shards(): return (lists[:, :K], lists[:, K:2 * K].astype(jnp.int32))  0.68 us

profile of v6, /device:TPU:64, one launch (start us, length us, event | category | flops | bytes accessed | tf_op | source)
XLA Modules:
  0.0 27.2 jit_solution(10739509301712786801)
XLA Ops:
  0.6 25.9 %shard_map.50 = f32[32,128]{1,0:T(8,128)S(1)} custom-call(bf16[128,768]{1,0:T(8,128)(2,1)} %q_ref.1, bf16[128,768]{1,0:T(8,128)(2,1)} %c_ref.1, s32[1,128]{1,0:T(1,128)} %bitcast.1), custom_call_target="tpu_custom_call" | custom-call | tf_op jit(solution)/shard_map/pallas_call | solution.py:451
  26.5 0.7 %slice_convert_fusion = (s32[32,32]{1,0:T(8,128)}, f32[32,32]{1,0:T(8,128)}) fusion(f32[32,128]{1,0:T(8,128)S(1)} %shard_map.50), kind=kLoop, calls=%fused_computation | loop fusion | flops 1024 | bytes 16384 | tf_op jit(solution)/shard_map/convert_element_type | solution.py:482

commit v7 on v6

--- a/solution.py
+++ b/solution.py
@@ -206,20 +206,6 @@
                     ring_sem.at[late - 4], inc=1, device_id=at(place - late, l | 1), device_id_type=MESH
                 )
 
-    own_q.wait()
-
-    @pl.when(early)
-    def _():
-        park_copy().start()
-
-    @pl.when(z > 0)
-    def _():
-        first_copy().start()
-
-    @when_z(4)
-    def _():
-        jump_copy().start()
-
     def across_copy(chunk, block):
         rows = pl.ds(*CAND_PIECES[chunk])
         return remote(
@@ -239,10 +225,34 @@
     def id_copy(k, block):
         return remote(id_ref, idents.at[block], id_send.at[k - 1], id_recv.at[k - 1], (i, l ^ k))
 
-    for k in (1, 2, 3):
-        id_copy(k, l).start()
-    for chunk in range(CAND_CHUNKS):
-        across_copy(chunk, l).start()
+    def offer():
+        for k in (1, 2, 3):
+            id_copy(k, l).start()
+        for chunk in range(CAND_CHUNKS):
+            across_copy(chunk, l).start()
+
+    @pl.when(~early)
+    def _():
+        offer()
+
+    own_q.wait()
+
+    @pl.when(early)
+    def _():
+        park_copy().start()
+
+    @pl.when(z > 0)
+    def _():
+        first_copy().start()
+
+    @when_z(4)
+    def _():
+        jump_copy().start()
+
+    @pl.when(early)
+    def _():
+        offer()
+
     beside_copy(l).start()
 
     @pl.when((z > 0) & (z < ROW - 1))

time: 27.3 us -> 27.3 us (level)
  no operation moved by 1% of the time
where the time goes in v7:
time: 27.3 us; the launch traced here: 27.2 us
  Pallas kernels  25.9 us (95%)
  other arithmetic  0.68 us (2%)
  between operations  0.64 us (2%)
    pallas_call x1, Pallas kernels, shards(): pl.pallas_call(kernel, out_shape=jax.ShapeDtypeStruct((ROWS, 128), jnp.fl...  25.9 us
    convert_element_type x1, other arithmetic, shards(): return (lists[:, :K], lists[:, K:2 * K].astype(jnp.int32))  0.68 us

profile of v7, /device:TPU:64, one launch (start us, length us, event | category | flops | bytes accessed | tf_op | source)
XLA Modules:
  0.0 27.2 jit_solution(6653835089651049507)
XLA Ops:
  0.6 25.9 %shard_map.50 = f32[32,128]{1,0:T(8,128)S(1)} custom-call(bf16[128,768]{1,0:T(8,128)(2,1)} %q_ref.1, bf16[128,768]{1,0:T(8,128)(2,1)} %c_ref.1, s32[1,128]{1,0:T(1,128)} %bitcast.1), custom_call_target="tpu_custom_call" | custom-call | tf_op jit(solution)/shard_map/pallas_call | solution.py:461
  26.5 0.7 %slice_convert_fusion = (s32[32,32]{1,0:T(8,128)}, f32[32,32]{1,0:T(8,128)}) fusion(f32[32,128]{1,0:T(8,128)S(1)} %shard_map.50), kind=kLoop, calls=%fused_computation | loop fusion | flops 1024 | bytes 16384 | tf_op jit(solution)/shard_map/convert_element_type | solution.py:492

commit v8 on v7

--- a/solution.py
+++ b/solution.py
@@ -372,9 +372,8 @@
 
         block = slots[s]
         four = jnp.concatenate([block] * 4, 0)
-        inner = by_layer(
-            [lax.dot_general(cands[m], four, NT, preferred_element_type=jnp.float32) for m in range(LAYERS)]
-        )
+        every = lax.dot_general(cands[...].reshape(LAYERS * CB, D), four, NT, preferred_element_type=jnp.float32)
+        inner = by_layer([every[CB * m : CB * m + CB] for m in range(LAYERS)])
         v = smallest(base[...] - inner.astype(jnp.int32) * 1024)
 
         @pl.when(s == 0)

time: 27.3 us -> 27.3 us (level)
  no operation moved by 1% of the time
where the time goes in v8:
time: 27.3 us; the launch traced here: 27.2 us
  Pallas kernels  25.9 us (95%)
  other arithmetic  0.68 us (2%)
  between operations  0.64 us (2%)
    pallas_call x1, Pallas kernels, shards(): pl.pallas_call(kernel, out_shape=jax.ShapeDtypeStruct((ROWS, 128), jnp.fl...  25.9 us
    convert_element_type x1, other arithmetic, shards(): return (lists[:, :K], lists[:, K:2 * K].astype(jnp.int32))  0.68 us

profile of v8, /device:TPU:64, one launch (start us, length us, event | category | flops | bytes accessed | tf_op | source)
XLA Modules:
  0.0 27.2 jit_solution(12774135700962331694)
XLA Ops:
  0.6 25.9 %shard_map.50 = f32[32,128]{1,0:T(8,128)S(1)} custom-call(bf16[128,768]{1,0:T(8,128)(2,1)} %q_ref.1, bf16[128,768]{1,0:T(8,128)(2,1)} %c_ref.1, s32[1,128]{1,0:T(1,128)} %bitcast.1), custom_call_target="tpu_custom_call" | custom-call | tf_op jit(solution)/shard_map/pallas_call | solution.py:460
  26.5 0.7 %slice_convert_fusion = (s32[32,32]{1,0:T(8,128)}, f32[32,32]{1,0:T(8,128)}) fusion(f32[32,128]{1,0:T(8,128)S(1)} %shard_map.50), kind=kLoop, calls=%fused_computation | loop fusion | flops 1024 | bytes 16384 | tf_op jit(solution)/shard_map/convert_element_type | solution.py:491
